TPU v7x, 512 devices: a whole 4x4x16 slice. The times are simulated.
512 devices in a mesh: segment: 16 (over z), expert: 32 (over y, x, core).
Axes of the slice: x: 4, y: 4, z: 16, core: 2. Of those that a mesh axis runs over, the one named last changes fastest.
Arguments:
- q_heads: bfloat16 [32, 2048, 1024], P('expert', 'segment'), may hold values from -6 to 6
- k_heads: bfloat16 [32, 2048, 1024], P('expert', 'segment'), may hold values from -6 to 6
- values: bfloat16 [32, 2048, 2048], P('expert', 'segment'), may hold values from -6 to 6
- beta: bfloat16 [32, 2048, 16], P('expert', 'segment'), may hold values from 0.049804688 to 0.94921875
- decay: bfloat16 [32, 2048, 16], P('expert', 'segment'), may hold values from -1 to 0
- head_gain: float32 [128], replicated, may hold values from 0.1 to 1.9
- suffix_len: int32 [32], P('expert'), may hold values from 256 to 2048, as said below
- store_states: bfloat16 [128, 16, 128, 128], P('expert', 'segment'), may hold values from -3 to 3
- cache_row: int32 [32], replicated, may hold values from 0 to 127
- write_slot: int32 [32], P('expert'), may hold values from 0 to 3
- expert_ids: int32 [32, 2048, 4], P('expert', 'segment'), may hold values from 0 to 511, all different within a row; in each aligned block of 128 rows (0 to 127, 128 to 255, ..., all dimensions but the last counted through in order) at most 2 rows name the same one
- route_weight: float32 [32, 2048, 4], P('expert', 'segment'), may hold values from 0.1 to 0.5
- w_gate: bfloat16 [512, 2048, 256], P(('segment', 'expert')), may hold values from -0.125 to 0.125
- w_up: bfloat16 [512, 2048, 256], P(('segment', 'expert')), may hold values from -0.125 to 0.125
- w_down: bfloat16 [512, 256, 2048], P(('segment', 'expert')), may hold values from -0.375 to 0.375
Outputs:
- mixed_out: bfloat16 [32, 2048, 2048], P('expert', 'segment')
- store_out: bfloat16 [128, 16, 128, 128], P('expert', 'segment')
Inputs may be any that keep to these rules, and one draw needn't show every extreme that they name: `expert_ids`: in the 128 positions of one device (aligned blocks of the request-major order) no expert is named by more than 2 routes, a bound that some block reaches. `suffix_len`: some request has exactly 2048.
All inputs are finite; a program needn't handle non-finite values.
Results may differ from a plain program's by a relative error of at most 0.0054.
Values may be sent and summed in bfloat16 or wider, within the bound.
A program may use at most 64 MiB of HBM per device.

v0:
```python
import jax
import jax.numpy as jnp
from jax import lax
from jax.sharding import PartitionSpec as P

BLOCK = 128
TOP = 4


def unit_rows(block, factor):
    squares = jnp.sum(block * block, axis=-1, keepdims=True)
    return block * lax.rsqrt(squares + 1e-06) * factor


def by_blocks(block, nblocks):
    return block.reshape(nblocks, BLOCK, block.shape[1], block.shape[2]).transpose(2, 0, 1, 3)


def unit_lower_inverse(lower_part, precise):
    nilpotent = -lower_part
    identity = jnp.eye(BLOCK, dtype=jnp.float32)
    inverse = identity + nilpotent
    power = nilpotent
    for level in range(BLOCK.bit_length() - 2):
        power = jnp.einsum("hnts,hnsu->hntu", power, power, precision=precise)
        inverse = inverse + jnp.einsum("hnts,hnsu->hntu", inverse, power, precision=precise)
    return inverse


def shards(
    q_heads,
    k_heads,
    values,
    beta,
    decay,
    head_gain,
    suffix_len,
    store_states,
    cache_row,
    write_slot,
    expert_ids,
    route_weight,
    w_gate,
    w_up,
    w_down,
):
    precise = lax.Precision.HIGHEST
    segments = lax.axis_size("segment")
    columns = lax.axis_size("expert")
    column = lax.axis_index("expert")
    tok_dev = q_heads.shape[1]
    heads_here = store_states.shape[1]
    key_dim = store_states.shape[2]
    head_total = values.shape[2] // key_dim
    repeat_count = head_total // (q_heads.shape[2] // key_dim)

    def widen(block):
        shaped = block[0].reshape(tok_dev, -1, key_dim)
        return jnp.repeat(shaped, repeat_count, axis=1).reshape(tok_dev, head_total * key_dim)

    packed = jnp.stack([widen(q_heads), widen(k_heads), values[0]])
    gating = jnp.stack([beta[0], decay[0]])
    packed, gating = (
        lax.all_to_all(packed, "segment", split_axis=2, concat_axis=1, tiled=True),
        lax.all_to_all(gating, "segment", split_axis=2, concat_axis=1, tiled=True),
    )
    suffix = packed.shape[1]
    nblocks = suffix // BLOCK
    my_row = cache_row[column]
    empty_state = jnp.zeros(store_states.shape[1:], jnp.bfloat16)
    piece = lax.all_gather(store_states, "expert", axis=0, tiled=True)
    inside = (my_row >= 0) & (my_row < piece.shape[0])
    taken = lax.dynamic_index_in_dim(
        piece, jnp.clip(my_row, 0, piece.shape[0] - 1), 0, keepdims=False
    )
    initial = jnp.where(inside, taken, empty_state)
    queries = by_blocks(
        unit_rows(
            packed[0].astype(jnp.float32).reshape(suffix, heads_here, key_dim), key_dim ** (-0.5)
        ),
        nblocks,
    )
    keys_unit = by_blocks(
        unit_rows(packed[1].astype(jnp.float32).reshape(suffix, heads_here, key_dim), 1.0), nblocks
    )
    values_f = by_blocks(
        packed[2].astype(jnp.float32).reshape(suffix, heads_here, key_dim), nblocks
    )
    valid = (jnp.arange(suffix, dtype=jnp.int32) < suffix_len[0]).astype(jnp.float32)
    strength = (
        (gating[0].astype(jnp.float32) * valid[:, None])
        .reshape(nblocks, BLOCK, heads_here)
        .transpose(2, 0, 1)
    )
    log_decay = (
        (gating[1].astype(jnp.float32) * valid[:, None])
        .reshape(nblocks, BLOCK, heads_here)
        .transpose(2, 0, 1)
    )
    cumulative = jnp.cumsum(log_decay, axis=-1)
    spread = cumulative[..., :, None] - cumulative[..., None, :]
    strict = jnp.tril(jnp.ones((BLOCK, BLOCK), bool), -1)
    inclusive = jnp.tril(jnp.ones((BLOCK, BLOCK), bool), 0)
    below = jnp.where(strict, jnp.exp(jnp.where(strict, spread, 0.0)), 0.0)
    upto = jnp.where(inclusive, jnp.exp(jnp.where(inclusive, spread, 0.0)), 0.0)
    key_gram = jnp.einsum("hnti,hnsi->hnts", keys_unit, keys_unit, precision=precise)
    lower_part = strength[..., None] * below * key_gram
    growth = jnp.exp(cumulative)
    targets = jnp.concatenate(
        [strength[..., None] * values_f, (strength * growth)[..., None] * keys_unit], axis=-1
    )
    inverse = unit_lower_inverse(lower_part, precise)
    solved = jnp.einsum("hnts,hnsj->hntj", inverse, targets, precision=precise)
    pseudo = solved[..., :key_dim]
    weights_wy = solved[..., key_dim:]
    tail_decay = jnp.exp(cumulative[..., -1:] - cumulative)
    keys_tail = keys_unit * tail_decay[..., None]
    transition = growth[..., -1][..., None, None] * jnp.eye(
        key_dim, dtype=jnp.float32
    ) - jnp.einsum("hnti,hntj->hnij", keys_tail, weights_wy, precision=precise)
    injection = jnp.einsum("hnti,hntj->hnij", keys_tail, pseudo, precision=precise)

    def advance(state, inputs):
        matrix, offset = inputs
        return (jnp.einsum("hij,hjk->hik", matrix, state, precision=precise) + offset, state)

    final_state, starts = lax.scan(
        advance,
        initial.astype(jnp.float32),
        (jnp.moveaxis(transition, 1, 0), jnp.moveaxis(injection, 1, 0)),
    )
    starts = jnp.moveaxis(starts, 0, 1)
    corrected = pseudo - jnp.einsum("hnti,hnij->hntj", weights_wy, starts, precision=precise)
    scores = upto * jnp.einsum("hnti,hnsi->hnts", queries, keys_unit, precision=precise)
    raw = growth[..., None] * jnp.einsum("hnti,hnij->hntj", queries, starts, precision=precise)
    raw = raw + jnp.einsum("hnts,hnsj->hntj", scores, corrected, precision=precise)
    raw = raw * valid.reshape(nblocks, BLOCK)[None, :, :, None]
    normed = raw * lax.rsqrt(jnp.mean(raw * raw, axis=-1, keepdims=True) + 1e-06) * head_gain
    mixed_heads = (
        normed.transpose(1, 2, 0, 3).reshape(suffix, heads_here * key_dim).astype(jnp.bfloat16)
    )
    store_out = lax.dynamic_update_index_in_dim(
        store_states, final_state.astype(jnp.bfloat16), write_slot[0], 0
    )
    mixed = lax.all_to_all(mixed_heads, "segment", split_axis=0, concat_axis=1, tiled=True)
    width = mixed.shape[1]
    routes = expert_ids[0].reshape(-1)
    order = jnp.arange(routes.shape[0], dtype=jnp.int32)
    earlier = (routes[:, None] == routes[None, :]) & (order[None, :] < order[:, None])
    ranks = jnp.sum(earlier.astype(jnp.int32), axis=1)
    capacity = max(2, 2 * tok_dev * TOP // (segments * columns))
    slot_of = (routes * capacity + ranks).reshape(tok_dev, TOP)
    slot_total = segments * columns * capacity
    placing = jnp.any(
        slot_of[None, :, :] == jnp.arange(slot_total, dtype=jnp.int32)[:, None, None], axis=-1
    ).astype(jnp.bfloat16)
    outgoing = (
        jnp.dot(placing, mixed, preferred_element_type=jnp.float32)
        .astype(jnp.bfloat16)
        .reshape(segments, columns, capacity, width)
    )
    arrived = lax.all_to_all(
        lax.all_to_all(outgoing, "segment", split_axis=0, concat_axis=0, tiled=True),
        "expert",
        split_axis=1,
        concat_axis=1,
        tiled=True,
    )
    rows = arrived.reshape(-1, width)
    gate_part = jnp.dot(rows, w_gate[0], preferred_element_type=jnp.float32)
    up_part = jnp.dot(rows, w_up[0], preferred_element_type=jnp.float32)
    hidden = (jax.nn.silu(gate_part) * up_part).astype(jnp.bfloat16)
    result = (
        jnp.dot(hidden, w_down[0], preferred_element_type=jnp.float32)
        .astype(jnp.bfloat16)
        .reshape(segments, columns, capacity, width)
    )
    returned = lax.all_to_all(
        lax.all_to_all(result, "segment", split_axis=0, concat_axis=0, tiled=True),
        "expert",
        split_axis=1,
        concat_axis=1,
        tiled=True,
    )
    returned = returned.reshape(-1, width)
    total = mixed.astype(jnp.float32)
    weights_here = route_weight[0]
    for route in range(TOP):
        total = total + weights_here[:, route : route + 1] * returned[slot_of[:, route]].astype(
            jnp.float32
        )
    return (total.astype(jnp.bfloat16)[None], store_out)


def solution(mesh):
    return jax.shard_map(
        shards,
        mesh=mesh,
        in_specs=(
            P("expert", "segment", None),
            P("expert", "segment", None),
            P("expert", "segment", None),
            P("expert", "segment", None),
            P("expert", "segment", None),
            P(),
            P("expert"),
            P("expert", "segment", None, None),
            P(),
            P("expert"),
            P("expert", "segment", None),
            P("expert", "segment", None),
            P(("segment", "expert"), None, None),
            P(("segment", "expert"), None, None),
            P(("segment", "expert"), None, None),
        ),
        out_specs=(P("expert", "segment", None), P("expert", "segment", None, None)),
        check_vma=False,
    )
```

profile of v0, /device:TPU:1, one launch (start us, length us, event | category | flops | bytes accessed | tf_op | source)
XLA Modules:
  0.0 860.4 jit_solution(7870385760820907862)
XLA Ops:
  7.2 1.7 copy.163
  10.8 15.7 %all-to-all-start = ((bf16[2,128,16]{1,0,2:T(2,128)(2,1)}), bf16[2,128,16]{1,0,2:T(2,128)(2,1)S(1)}, u32[]{:S(2)}, u32[]{:S(2)}) async-start(bf16[2,128,16]{1,0,2:T(2,128)(2,1)} %pad_maximum_fusion.1), calls=%async_computation | async-start | bytes 16384 | tf_op jit(solution)/shard_map/all_to_all | solution.py:65
  28.9 1.3 copy.120
  30.6 10.8 %copy.121 = bf16[3,128,2048]{1,0,2:T(4,128)(2,1)} copy(bf16[3,128,2048]{1,2,0:T(8,128)(2,1)S(1)} %pad_maximum_fusion) | data formatting | bytes 3145728 | tf_op jit(solution)/shard_map/stack | solution.py:61
  41.3 11.6 %all-to-all-start.1 = ((bf16[3,128,2048]{1,0,2:T(4,128)(2,1)}), bf16[3,128,2048]{1,0,2:T(4,128)(2,1)S(1)}, u32[]{:S(2)}, u32[]{:S(2)}) async-start(bf16[3,128,2048]{1,0,2:T(4,128)(2,1)} %copy.121), calls=%async_computation.1 | async-start | bytes 4194304 | tf_op jit(solution)/shard_map/all_to_all | solution.py:64
  57.6 87.2 %all-to-all-done.1 = bf16[3,128,2048]{1,0,2:T(4,128)(2,1)S(1)} async-done(((bf16[3,128,2048]{1,0,2:T(4,128)(2,1)}), bf16[3,128,2048]{1,0,2:T(4,128)(2,1)S(1)}, u32[]{:S(2)}, u32[]{:S(2)}) %all-to-all-start.1) | async-done | bytes 1572896 | tf_op jit(solution)/shard_map/all_to_all | solution.py:64
  144.8 1.3 copy-done.2
  146.1 3.0 copy.123
  149.7 2.6 fusion.12
  152.4 1.2 convert_multiply_fusion.8
  157.0 1.3 convolution_add_fusion.6
  158.3 1.2 convolution_add_fusion.5
  160.7 1.2 convolution_add_fusion.4
  163.0 1.2 convolution_add_fusion.3
  165.4 1.6 convolution_add_fusion.2
  167.0 1.2 convolution_add_fusion.1
  168.2 1.9 fusion.9
  170.1 3.5 convolution_bitcast_fusion.1
  173.7 3.4 fusion.11
  177.1 3.5 convolution_multiply_fusion.1
  181.4 28.0 %while.12 = (s32[]{:T(128)}, f32[1,128,128]{2,1,0:T(8,128)S(1)}, f32[16,1,128,128]{3,2,1,0:T(8,128)}, f32[16,1,128,128]{3,2,1,0:T(8,128)}, f32[16,1,128,128]{3,2,1,0:T(8,128)}, /*index=5*/s32[]{:T(128)}) while((s32[]{:T(128)}, f32[1,128,128]{2,1,0:T(8,128)S(1)}, f32[16,1,128,128]{3,2,1,0:T(8,128)}, f32[16,1,128,128]{3,2,1,0:T(8,128)}, ...), condition=%wide.region_4.5_spmd, body=%wide.region_3.4_spmd.sunk | while | flops 25182208 | bytes 525893 | solution.py:127
  209.4 3.2 fusion.14
  212.6 2.2 convolution_multiply_fusion.2
  214.8 1.9 multiply_reduce_fusion
  217.8 11.1 %all-to-all-start.2 = ((bf16[16,128,128]{1,2,0:T(8,128)(2,1)}), bf16[16,128,128]{1,2,0:T(8,128)(2,1)S(1)}, u32[]{:S(2)}, u32[]{:S(2)}) async-start(bf16[16,128,128]{1,2,0:T(8,128)(2,1)} %multiply_convert_fusion), calls=%async_computation.2 | async-start | bytes 1048576 | tf_op jit(solution)/shard_map/all_to_all | solution.py:145
  230.0 21.8 %all-to-all-done.2 = bf16[16,128,128]{1,2,0:T(8,128)(2,1)S(1)} async-done(((bf16[16,128,128]{1,2,0:T(8,128)(2,1)}), bf16[16,128,128]{1,2,0:T(8,128)(2,1)S(1)}, u32[]{:S(2)}, u32[]{:S(2)}) %all-to-all-start.2) | async-done | bytes 524320 | tf_op jit(solution)/shard_map/all_to_all | solution.py:145
  251.8 3.2 convolution_convert_fusion.1
  254.9 7.6 reshape.631
  262.6 192.9 %all_to_all.66 = bf16[16,32,2,2048]{3,2,1,0:T(2,128)(2,1)S(1)} all-to-all(bf16[16,32,2,2048]{3,2,1,0:T(2,128)(2,1)} %reshape.631), channel_id=1, replica_groups=mesh['segment'=16,'expert'=32] {'segment'}, dimensions={0} | all-to-all | bytes 8388608 | tf_op jit(solution)/shard_map/all_to_all | solution.py:163
  455.4 6.5 copy.133
  461.9 65.4 %all_to_all.67 = bf16[16,32,2,2048]{3,2,0,1:T(2,128)(2,1)S(1)} all-to-all(bf16[16,32,2,2048]{3,2,0,1:T(2,128)(2,1)} %copy.133), channel_id=1, replica_groups=mesh['segment'=16,'expert'=32] {'expert'}, dimensions={1} | all-to-all | bytes 8388608 | tf_op jit(solution)/shard_map/all_to_all | solution.py:162
  527.3 6.0 copy.134
  533.3 7.2 reshape.632
  540.6 4.8 fusion.43
  545.4 9.1 %convolution_convert_fusion = bf16[1024,2048]{1,0:T(8,128)(2,1)} fusion(bf16[1024,2048]{1,0:T(8,128)(2,1)} %reshape.632, bf16[1,256,2048]{2,1,0:T(8,128)(2,1)S(1)} %copy-done, bf16[1,2048,256]{2,1,0:T(8,128)(2,1)} %param.30, f32[1024,256]{1,0:T(8,128)} %fusion.43), kind=kOutput, calls=%fused_computation.11 | convolution fusion | flops 2151153664 | bytes 11534336 | tf_op jit(solution)/shard_map/dot_general | solution.py:174
  554.5 7.6 reshape.633
  562.1 186.0 %all_to_all.68 = bf16[16,32,2,2048]{3,2,1,0:T(2,128)(2,1)S(1)} all-to-all(bf16[16,32,2,2048]{3,2,1,0:T(2,128)(2,1)} %reshape.633), channel_id=1, replica_groups=mesh['segment'=16,'expert'=32] {'segment'}, dimensions={0} | all-to-all | bytes 8388608 | tf_op jit(solution)/shard_map/all_to_all | solution.py:179
  748.1 6.5 copy.135
  754.6 12.3 %all-to-all-start.6 = ((bf16[16,32,2,2048]{3,2,0,1:T(2,128)(2,1)}), bf16[16,32,2,2048]{3,2,0,1:T(2,128)(2,1)}, u32[]{:S(2)}, u32[]{:S(2)}) async-start(bf16[16,32,2,2048]{3,2,0,1:T(2,128)(2,1)} %copy.135), calls=%async_computation.6 | async-start | bytes 8388608 | tf_op jit(solution)/shard_map/all_to_all | solution.py:178
  769.8 1.6 copy.137
  771.4 45.7 %all-to-all-done.6 = bf16[16,32,2,2048]{3,2,0,1:T(2,128)(2,1)} async-done(((bf16[16,32,2,2048]{3,2,0,1:T(2,128)(2,1)}), bf16[16,32,2,2048]{3,2,0,1:T(2,128)(2,1)}, u32[]{:S(2)}, u32[]{:S(2)}) %all-to-all-start.6) | async-done | bytes 4194336 | tf_op jit(solution)/shard_map/all_to_all | solution.py:178
  817.1 8.0 copy.136
  825.1 7.2 reshape.634
  832.3 4.2 gather_fusion
  836.5 4.2 gather_fusion.1
  840.7 5.0 gather_fusion.2
  845.6 5.0 gather_fusion.3
  850.6 2.5 fusion.36
  (119 shorter events, 46.6 us)
Async XLA Ops:
  7.2 538.2 %copy-start = (bf16[1,256,2048]{2,1,0:T(8,128)(2,1)S(1)}, bf16[1,256,2048]{2,1,0:T(8,128)(2,1)}, u32[]{:S(2)}) copy-start(bf16[1,256,2048]{2,1,0:T(8,128)(2,1)} %param.31) | copy-start | bytes 3145732
  10.8 30.5 %all-to-all-start = ((bf16[2,128,16]{1,0,2:T(2,128)(2,1)}), bf16[2,128,16]{1,0,2:T(2,128)(2,1)S(1)}, u32[]{:S(2)}, u32[]{:S(2)}) async-start(bf16[2,128,16]{1,0,2:T(2,128)(2,1)} %pad_maximum_fusion.1), calls=%async_computation | async-start | bytes 16384 | tf_op jit(solution)/shard_map/all_to_all | solution.py:65
  41.3 12.3 %copy-start.8 = (s32[32]{0:T(128)S(1)}, s32[32]{0:T(128)}, u32[]{:S(2)}) copy-start(s32[32]{0:T(128)} %param.25) | copy-start | bytes 388
  41.3 103.4 %all-to-all-start.1 = ((bf16[3,128,2048]{1,0,2:T(4,128)(2,1)}), bf16[3,128,2048]{1,0,2:T(4,128)(2,1)S(1)}, u32[]{:S(2)}, u32[]{:S(2)}) async-start(bf16[3,128,2048]{1,0,2:T(4,128)(2,1)} %copy.121), calls=%async_computation.1 | async-start | bytes 4194304 | tf_op jit(solution)/shard_map/all_to_all | solution.py:64
  52.9 127.7 %all-gather.2.cloned.1.call-start = ((), (), s32[]{:S(2)}) async-start(), calls=%async_computation.7 | async-start | bytes 4325376 | tf_op jit(solution)/shard_map/all_gather | solution.py:71
  144.8 1.3 copy-start.2
  170.1 7.0 copy-start.1
  209.4 3.2 copy-start.3
  212.6 2.3 copy-start.4
  214.8 2.0 copy-start.7
  216.8 12.2 %copy-start.5 = (s32[1,128,4]{1,2,0:T(4,128)S(1)}, s32[1,128,4]{1,2,0:T(4,128)}, u32[]{:S(2)}) copy-start(s32[1,128,4]{1,2,0:T(4,128)} %param.27) | copy-start | bytes 6148
  217.8 34.0 %all-to-all-start.2 = ((bf16[16,128,128]{1,2,0:T(8,128)(2,1)}), bf16[16,128,128]{1,2,0:T(8,128)(2,1)S(1)}, u32[]{:S(2)}, u32[]{:S(2)}) async-start(bf16[16,128,128]{1,2,0:T(8,128)(2,1)} %multiply_convert_fusion), calls=%async_computation.2 | async-start | bytes 1048576 | tf_op jit(solution)/shard_map/all_to_all | solution.py:145
  754.6 13.4 %copy-start.6 = (f32[1,128,4]{1,2,0:T(4,128)S(1)}, f32[1,128,4]{1,2,0:T(4,128)}, u32[]{:S(2)}) copy-start(f32[1,128,4]{1,2,0:T(4,128)} %param.28) | copy-start | bytes 6148
  754.6 62.4 %all-to-all-start.6 = ((bf16[16,32,2,2048]{3,2,0,1:T(2,128)(2,1)}), bf16[16,32,2,2048]{3,2,0,1:T(2,128)(2,1)}, u32[]{:S(2)}, u32[]{:S(2)}) async-start(bf16[16,32,2,2048]{3,2,0,1:T(2,128)(2,1)} %copy.135), calls=%async_computation.6 | async-start | bytes 8388608 | tf_op jit(solution)/shard_map/all_to_all | solution.py:178
Sparse Core Ops, SparseCore 0:
  57.5 63.9 all-gather.1
where the time goes:
time: 872 us; the launch traced here: 860 us
  blocking collectives  444 us (51%)
  waiting for transfers between devices  155 us (18%)
  local copies, waits for them, and re-layouts  110 us (13%)
  matrix products  71.1 us (8%)
  starting transfers between devices  50.8 us (6%)
  between operations  18 us (2%)
  other arithmetic  10.1 us (1%)
    all_to_all x1, blocking collectives, shards(): lax.all_to_all(outgoing, 'segment', split_axis=0, concat_axis=0, tiled=True)  193 us
    all_to_all x1, blocking collectives, shards(): lax.all_to_all(result, 'segment', split_axis=0, concat_axis=0, tiled=True)  186 us
    all_to_all x1, waiting for transfers between devices, shards(): lax.all_to_all(packed, 'segment', split_axis=2, concat_axis=1, tiled=True)  87.2 us
    all_to_all x1, blocking collectives, shards(): lax.all_to_all(lax.all_to_all(outgoing, 'segment', split_axis=0, concat_a...  65.4 us
    all_to_all x1, waiting for transfers between devices, shards(): lax.all_to_all(lax.all_to_all(result, 'segment', split_axis=0, concat_axi...  45.7 us
    all_to_all x1, waiting for transfers between devices, shards(): lax.all_to_all(mixed_heads, 'segment', split_axis=0, concat_axis=1, tiled...  21.8 us
    gather x4, local copies, waits for them, and re-layouts, shards(): returned[slot_of[:, route]].astype(jnp.float32)  18.3 us
  transfers between devices with their start and end apart: 5, of which 3 were waited for; matrix products, arithmetic and copies ran while one was open for 6% of the time, Pallas kernels for 0%

commit v1 on v0

--- a/solution.py
+++ b/solution.py
@@ -1,10 +1,12 @@
 import jax
 import jax.numpy as jnp
 from jax import lax
+from jax.experimental import pallas as pl
+from jax.experimental.pallas import tpu as pltpu
 from jax.sharding import PartitionSpec as P
 
 BLOCK = 128
-TOP = 4
+MESH = pl.DeviceIdType.MESH
 
 
 def unit_rows(block, factor):
@@ -25,6 +27,363 @@
         power = jnp.einsum("hnts,hnsu->hntu", power, power, precision=precise)
         inverse = inverse + jnp.einsum("hnts,hnsu->hntu", inverse, power, precision=precise)
     return inverse
+
+
+def moe_kernel(
+    idx_ref,
+    rows_ref,
+    base_ref,
+    mix_ref,
+    gate_ref,
+    up_ref,
+    down_ref,
+    out_ref,
+    climb,
+    sink,
+    pick,
+    stage,
+    arrive,
+    back,
+    flat,
+    sum_up,
+    sum_down,
+    got_up,
+    got_down,
+    tall,
+    wide,
+    climb_send,
+    climb_recv,
+    sink_send,
+    sink_recv,
+    stage_send,
+    arrive_recv,
+    back_send,
+    back_recv,
+    up_send,
+    up_recv,
+    down_send,
+    down_recv,
+):
+    segments = lax.axis_size("segment")
+    columns = lax.axis_size("expert")
+    pairs = segments // 2
+    tok = rows_ref.shape[0]
+    heads = rows_ref.shape[1]
+    lane = rows_ref.shape[2]
+    half = tok // 2
+    seg = lax.axis_index("segment")
+    col = lax.axis_index("expert")
+    above = lax.rem(seg + 1, segments)
+    below = lax.rem(seg + segments - 1, segments)
+
+    barrier = pltpu.get_barrier_semaphore()
+
+    def greet(step, carry):
+        other = lax.rem(col + step, columns)
+        pl.semaphore_signal(barrier, inc=1, device_id=(seg, other), device_id_type=MESH)
+        return carry
+
+    lax.fori_loop(1, columns, greet, 0)
+    pl.semaphore_signal(barrier, inc=1, device_id=(above, col), device_id_type=MESH)
+    pl.semaphore_signal(barrier, inc=1, device_id=(below, col), device_id_type=MESH)
+    pl.semaphore_wait(barrier, columns + 1)
+
+    def part(ref, h):
+        return ref.at[pl.ds(h * half, half)]
+
+    def climb_copy(source, slot, h):
+        return pltpu.make_async_remote_copy(
+            src_ref=part(source, h),
+            dst_ref=part(climb.at[slot], h),
+            send_sem=climb_send.at[slot, h],
+            recv_sem=climb_recv.at[slot, h],
+            device_id=(above, col),
+            device_id_type=MESH,
+        )
+
+    def sink_copy(source, slot, h):
+        return pltpu.make_async_remote_copy(
+            src_ref=part(source, h),
+            dst_ref=part(sink.at[slot], h),
+            send_sem=sink_send.at[slot, h],
+            recv_sem=sink_recv.at[slot, h],
+            device_id=(below, col),
+            device_id_type=MESH,
+        )
+
+    for h in range(2):
+        climb_copy(rows_ref, 0, h).start()
+        sink_copy(rows_ref, 1, h).start()
+    sink[0] = rows_ref[...]
+
+    def rows_to_wide(rows):
+        tall[...] = rows.reshape(tok * heads, lane).astype(jnp.float32)
+        for j in range(heads):
+            wide[:, j * lane : (j + 1) * lane] = tall[pl.ds(j, tok, stride=heads), :].astype(
+                jnp.bfloat16
+            )
+
+    def send_out(source, target, send_sem, recv_sem, p, i):
+        other = lax.rem(col + i, columns)
+
+        @pl.when(i == 0)
+        def _():
+            pltpu.make_async_copy(source.at[p, col], target.at[p, col], recv_sem.at[p]).start()
+
+        @pl.when(i > 0)
+        def _():
+            pltpu.make_async_remote_copy(
+                src_ref=source.at[p, other],
+                dst_ref=target.at[p, col],
+                send_sem=send_sem.at[p],
+                recv_sem=recv_sem.at[p],
+                device_id=(seg, other),
+                device_id_type=MESH,
+            ).start()
+
+    def wait_all(target, sem, p):
+        pltpu.make_async_copy(target.at[p], target.at[p], sem.at[p]).wait()
+
+    def wait_sent(source, sem, p):
+        piece = source.at[p, pl.ds(0, columns - 1)]
+        pltpu.make_async_copy(piece, piece, sem.at[p]).wait()
+
+    def dispatch(p):
+        pick[0] = sink[p]
+        pick[1] = climb[p]
+
+        def one(i, carry):
+            other = lax.rem(col + i, columns)
+            for r in range(4):
+                stage[p, other, r] = pick[r // 2, idx_ref[p, other, r]]
+            send_out(stage, arrive, stage_send, arrive_recv, p, i)
+            return carry
+
+        lax.fori_loop(0, columns, one, 0)
+
+    def experts(p):
+        wait_all(arrive, arrive_recv, p)
+        wait_sent(stage, stage_send, p)
+        rows_to_wide(arrive[p].reshape(tok, heads, lane))
+        gate_part = jnp.dot(wide[...], gate_ref[...], preferred_element_type=jnp.float32)
+        up_part = jnp.dot(wide[...], up_ref[...], preferred_element_type=jnp.float32)
+        hidden = (gate_part * jax.nn.sigmoid(gate_part) * up_part).astype(jnp.bfloat16)
+        for j in range(heads):
+            tall[pl.ds(j, tok, stride=heads), :] = jnp.dot(
+                hidden,
+                down_ref[:, j * lane : (j + 1) * lane],
+                preferred_element_type=jnp.float32,
+            )
+        stage[p] = tall[...].astype(jnp.bfloat16).reshape(columns, 4, heads, lane)
+
+        def one(i, carry):
+            send_out(stage, back, back_send, back_recv, p, i)
+            return carry
+
+        lax.fori_loop(0, columns, one, 0)
+
+    def land(p):
+        wait_all(back, back_recv, p)
+        rows_to_wide(back[p].reshape(tok, heads, lane))
+        flat[p] = wide[...]
+
+    def gather_step(p, carry):
+        for h in range(2):
+            climb_copy(rows_ref, p, h).wait_recv()
+
+            @pl.when(p < pairs - 1)
+            def _():
+                climb_copy(climb.at[p], p + 1, h).start()
+
+            @pl.when(p >= 1)
+            def _():
+                sink_copy(rows_ref, p, h).wait_recv()
+
+                @pl.when(p < pairs - 1)
+                def _():
+                    sink_copy(sink.at[p], p + 1, h).start()
+
+        dispatch(p)
+
+        @pl.when(p >= 1)
+        def _():
+            experts(p - 1)
+
+        @pl.when(p >= 2)
+        def _():
+            land(p - 2)
+
+        return carry
+
+    lax.fori_loop(0, pairs, gather_step, 0)
+    experts(pairs - 1)
+    land(pairs - 2)
+    land(pairs - 1)
+
+    def term(p, source, h):
+        weights = mix_ref[p, source, pl.ds(h * half, half), :]
+        rows = flat[p]
+        slots = rows.shape[0]
+        return jnp.dot(
+            weights[:, :slots], rows, preferred_element_type=jnp.float32
+        ) + jnp.dot(weights[:, slots:], rows, preferred_element_type=jnp.float32)
+
+    def up_copy(i, h):
+        return pltpu.make_async_remote_copy(
+            src_ref=part(sum_up.at[i], h),
+            dst_ref=part(got_up.at[i], h),
+            send_sem=up_send.at[i, h],
+            recv_sem=up_recv.at[i, h],
+            device_id=(above, col),
+            device_id_type=MESH,
+        )
+
+    def down_copy(i, h):
+        return pltpu.make_async_remote_copy(
+            src_ref=part(sum_down.at[i], h),
+            dst_ref=part(got_down.at[i], h),
+            send_sem=down_send.at[i, h],
+            recv_sem=down_recv.at[i, h],
+            device_id=(below, col),
+            device_id_type=MESH,
+        )
+
+    for h in range(2):
+        spot = pl.ds(h * half, half)
+        sum_up[0, spot] = term(pairs - 1, 1, h).astype(jnp.bfloat16)
+        up_copy(0, h).start()
+        sum_down[0, spot] = term(pairs - 2, 1, h).astype(jnp.bfloat16)
+        down_copy(0, h).start()
+
+    def reduce_step(i, carry):
+        for h in range(2):
+            spot = pl.ds(h * half, half)
+            mine = term(pairs - i, 0, h)
+            up_copy(i - 1, h).wait_recv()
+            sum_up[i, spot] = (mine + got_up[i - 1, spot].astype(jnp.float32)).astype(jnp.bfloat16)
+            up_copy(i, h).start()
+
+            @pl.when(i < pairs - 1)
+            def _():
+                mine = term(pairs - 2 - i, 1, h)
+                down_copy(i - 1, h).wait_recv()
+                sum_down[i, spot] = (mine + got_down[i - 1, spot].astype(jnp.float32)).astype(
+                    jnp.bfloat16
+                )
+                down_copy(i, h).start()
+
+        return carry
+
+    lax.fori_loop(1, pairs, reduce_step, 0)
+    for h in range(2):
+        spot = pl.ds(h * half, half)
+        total = base_ref[spot, :].astype(jnp.float32) + term(0, 0, h)
+        down_copy(pairs - 2, h).wait_recv()
+        total = total + got_down[pairs - 2, spot].astype(jnp.float32)
+        up_copy(pairs - 1, h).wait_recv()
+        total = total + got_up[pairs - 1, spot].astype(jnp.float32)
+        out_ref[spot, :] = total.astype(jnp.bfloat16)
+
+    def drain(p, carry):
+        wait_sent(stage, back_send, p)
+        for h in range(2):
+            climb_copy(rows_ref, p, h).wait_send()
+            up_copy(p, h).wait_send()
+
+            @pl.when(p >= 1)
+            def _():
+                sink_copy(rows_ref, p, h).wait_send()
+                down_copy(p - 1, h).wait_send()
+
+        return carry
+
+    lax.fori_loop(0, pairs, drain, 0)
+
+
+def moe(idx, rows, base, mix, w_gate, w_up, w_down):
+    segments = lax.axis_size("segment")
+    columns = lax.axis_size("expert")
+    pairs = segments // 2
+    tok, heads, lane = rows.shape
+    width = base.shape[1]
+    slots = columns * 4
+    bf = jnp.bfloat16
+    dma = pltpu.SemaphoreType.DMA
+    whole = pl.BlockSpec(memory_space=pltpu.VMEM)
+    return pl.pallas_call(
+        moe_kernel,
+        out_shape=jax.ShapeDtypeStruct((tok, width), bf),
+        in_specs=[pl.BlockSpec(memory_space=pltpu.SMEM)] + [whole] * 6,
+        out_specs=whole,
+        scratch_shapes=[
+            pltpu.VMEM((pairs, tok, heads, lane), bf),
+            pltpu.VMEM((pairs, tok, heads, lane), bf),
+            pltpu.VMEM((2, tok, heads, lane), bf),
+            pltpu.VMEM((pairs, columns, 4, heads, lane), bf),
+            pltpu.VMEM((pairs, columns, 4, heads, lane), bf),
+            pltpu.VMEM((pairs, columns, 4, heads, lane), bf),
+            pltpu.VMEM((pairs, slots, width), bf),
+            pltpu.VMEM((pairs, tok, width), bf),
+            pltpu.VMEM((pairs - 1, tok, width), bf),
+            pltpu.VMEM((pairs, tok, width), bf),
+            pltpu.VMEM((pairs - 1, tok, width), bf),
+            pltpu.VMEM((tok * heads, lane), jnp.float32),
+            pltpu.VMEM((tok, width), bf),
+            dma((pairs, 2)),
+            dma((pairs, 2)),
+            dma((pairs, 2)),
+            dma((pairs, 2)),
+            dma((pairs,)),
+            dma((pairs,)),
+            dma((pairs,)),
+            dma((pairs,)),
+            dma((pairs, 2)),
+            dma((pairs, 2)),
+            dma((pairs - 1, 2)),
+            dma((pairs - 1, 2)),
+        ],
+        compiler_params=pltpu.CompilerParams(
+            collective_id=1, has_side_effects=True, vmem_limit_bytes=60 * 1024 * 1024
+        ),
+    )(idx, rows, base, mix, w_gate, w_up, w_down)
+
+
+def route_tables(expert_ids, route_weight):
+    segments = lax.axis_size("segment")
+    columns = lax.axis_size("expert")
+    seg = lax.axis_index("segment")
+    pairs = segments // 2
+    tok, top = expert_ids.shape
+    routes = jnp.concatenate([expert_ids.T.astype(jnp.float32), route_weight.T], axis=0)
+    routes = lax.all_gather(routes, "segment", axis=0, tiled=False)
+    step = jnp.arange(pairs, dtype=jnp.int32)
+    place = jnp.stack([seg + step, seg + segments - 1 - step], axis=1) % segments
+    routes = routes[place]
+    here = (seg * columns + jnp.arange(columns, dtype=jnp.int32)).astype(jnp.float32)
+    same = routes[:, :, None, :top, :] == here[None, None, :, None, None]
+    weight = jnp.sum(jnp.where(same, routes[:, :, None, top:, :], 0.0), axis=3)
+    named = jnp.any(same, axis=3)
+    token = jnp.arange(tok, dtype=jnp.int32)
+    first = jnp.min(jnp.where(named, token, tok), axis=-1)
+    last = jnp.max(jnp.where(named, token, -1), axis=-1)
+    index = jnp.stack([first % tok, jnp.maximum(last, 0)], axis=-1)
+    index = index.transpose(0, 2, 1, 3).reshape(pairs, columns, 4)
+    at_first = jnp.where(token == first[..., None], weight, 0.0)
+    at_last = jnp.where((token == last[..., None]) & (last != first)[..., None], weight, 0.0)
+    both = jnp.stack([at_first, at_last], axis=3)
+    none = jnp.zeros_like(both[:, 0])
+    mix = jnp.stack(
+        [
+            jnp.concatenate([both[:, 0], none], axis=2),
+            jnp.concatenate([none, both[:, 1]], axis=2),
+        ],
+        axis=1,
+    )
+    mix = mix.reshape(pairs, 2, columns * 4, tok).transpose(0, 1, 3, 2)
+    high = lax.reduce_precision(mix, 8, 7)
+    low = lax.reduce_precision(mix - high, 8, 7)
+    mix = jnp.concatenate([high, low], axis=-1).astype(jnp.bfloat16)
+    return index, mix
 
 
 def shards(
@@ -143,53 +502,10 @@
         store_states, final_state.astype(jnp.bfloat16), write_slot[0], 0
     )
     mixed = lax.all_to_all(mixed_heads, "segment", split_axis=0, concat_axis=1, tiled=True)
-    width = mixed.shape[1]
-    routes = expert_ids[0].reshape(-1)
-    order = jnp.arange(routes.shape[0], dtype=jnp.int32)
-    earlier = (routes[:, None] == routes[None, :]) & (order[None, :] < order[:, None])
-    ranks = jnp.sum(earlier.astype(jnp.int32), axis=1)
-    capacity = max(2, 2 * tok_dev * TOP // (segments * columns))
-    slot_of = (routes * capacity + ranks).reshape(tok_dev, TOP)
-    slot_total = segments * columns * capacity
-    placing = jnp.any(
-        slot_of[None, :, :] == jnp.arange(slot_total, dtype=jnp.int32)[:, None, None], axis=-1
-    ).astype(jnp.bfloat16)
-    outgoing = (
-        jnp.dot(placing, mixed, preferred_element_type=jnp.float32)
-        .astype(jnp.bfloat16)
-        .reshape(segments, columns, capacity, width)
-    )
-    arrived = lax.all_to_all(
-        lax.all_to_all(outgoing, "segment", split_axis=0, concat_axis=0, tiled=True),
-        "expert",
-        split_axis=1,
-        concat_axis=1,
-        tiled=True,
-    )
-    rows = arrived.reshape(-1, width)
-    gate_part = jnp.dot(rows, w_gate[0], preferred_element_type=jnp.float32)
-    up_part = jnp.dot(rows, w_up[0], preferred_element_type=jnp.float32)
-    hidden = (jax.nn.silu(gate_part) * up_part).astype(jnp.bfloat16)
-    result = (
-        jnp.dot(hidden, w_down[0], preferred_element_type=jnp.float32)
-        .astype(jnp.bfloat16)
-        .reshape(segments, columns, capacity, width)
-    )
-    returned = lax.all_to_all(
-        lax.all_to_all(result, "segment", split_axis=0, concat_axis=0, tiled=True),
-        "expert",
-        split_axis=1,
-        concat_axis=1,
-        tiled=True,
-    )
-    returned = returned.reshape(-1, width)
-    total = mixed.astype(jnp.float32)
-    weights_here = route_weight[0]
-    for route in range(TOP):
-        total = total + weights_here[:, route : route + 1] * returned[slot_of[:, route]].astype(
-            jnp.float32
-        )
-    return (total.astype(jnp.bfloat16)[None], store_out)
+    index, mix = route_tables(expert_ids[0], route_weight[0])
+    rows = mixed.reshape(tok_dev, head_total, key_dim)
+    out = moe(index, rows, mixed, mix, w_gate[0], w_up[0], w_down[0])
+    return (out[None], store_out)
 
 
 def solution(mesh):

time: 872 us -> 502 us (0.58)
  blocking collectives: 444 us -> 106 us
  Pallas kernels: 0 us -> 227 us
  waiting for transfers between devices: 155 us -> 13.6 us
  local copies, waits for them, and re-layouts: 110 us -> 28.8 us
  matrix products: 71.1 us -> 53.6 us
  starting transfers between devices: 50.8 us -> 38.2 us
    all_to_all x3 -> x0, blocking collectives: 444 us -> none  [the longest x1 193 us: shards(): lax.all_to_all(outgoing, 'segment', split_axis=0, concat_axis=0, tiled=True)]
    pallas_call x0 -> x1, Pallas kernels: none -> 227 us  [moe(): pl.pallas_call(moe_kernel, out_shape=jax.ShapeDtypeStruct((tok, width), b...]
    all_gather x0 -> x1, blocking collectives: none -> 106 us  [route_tables(): routes = lax.all_gather(routes, 'segment', axis=0, tiled=False)]
    all_to_all x1, waiting for transfers between devices: 87.2 us -> 0.01 us  [shards(): lax.all_to_all(packed, 'segment', split_axis=2, concat_axis=1, tiled=True)]
    all_to_all x1 -> x0, waiting for transfers between devices: 45.7 us -> none  [shards(): lax.all_to_all(lax.all_to_all(result, 'segment', split_axis=0, concat_axi...]
    reshape x4 -> x1, local copies, waits for them, and re-layouts: 29.7 us -> 0.8 us  [route_tables(): index = index.transpose(0, 2, 1, 3).reshape(pairs, columns, 4)]
    all_to_all x4 -> x1, local copies, waits for them, and re-layouts: 27 us -> 0.34 us  [shards(): lax.all_to_all(mixed_heads, 'segment', split_axis=0, concat_axis=1, tiled...]
    gather x4 -> x1, local copies, waits for them, and re-layouts: 18.3 us -> 0.56 us  [route_tables(): routes = routes[place]]
  transfers between devices with their start and end apart: 5 -> 4, of which waited for: 3 -> 1; matrix products, arithmetic and copies ran while one was open for 6% -> 11% of each run, Pallas kernels for 0% -> 0%
where the time goes in v1:
time: 502 us; the launch traced here: 493 us
  Pallas kernels  227 us (45%)
  blocking collectives  106 us (21%)
  matrix products  53.6 us (11%)
  starting transfers between devices  38.2 us (8%)
  local copies, waits for them, and re-layouts  28.8 us (6%)
  between operations  18.3 us (4%)
  waiting for transfers between devices  13.6 us (3%)
  other arithmetic  7.46 us (1%)
    pallas_call x1, Pallas kernels, moe(): pl.pallas_call(moe_kernel, out_shape=jax.ShapeDtypeStruct((tok, width), b...  227 us
    all_gather x1, blocking collectives, route_tables(): routes = lax.all_gather(routes, 'segment', axis=0, tiled=False)  106 us
    dot_general x16, matrix products, advance(): jnp.einsum('hij,hjk->hik', matrix, state, precision=precise) + offset  17.3 us
    all_to_all x1, starting transfers between devices, shards(): lax.all_to_all(gating, 'segment', split_axis=2, concat_axis=1, tiled=True)  15.7 us
    all_to_all x1, waiting for transfers between devices, shards(): lax.all_to_all(mixed_heads, 'segment', split_axis=0, concat_axis=1, tiled...  12.9 us
    all_to_all x1, starting transfers between devices, shards(): lax.all_to_all(packed, 'segment', split_axis=2, concat_axis=1, tiled=True)  11.6 us
    all_to_all x1, starting transfers between devices, shards(): lax.all_to_all(mixed_heads, 'segment', split_axis=0, concat_axis=1, tiled...  10.8 us
    another operation x1, local copies, waits for them, and re-layouts, shards(): packed = jnp.stack([widen(q_heads), widen(k_heads), values[0]])  10.8 us
  transfers between devices with their start and end apart: 4, of which 1 were waited for; matrix products, arithmetic and copies ran while one was open for 11% of the time, Pallas kernels for 0%

profile of v1, /device:TPU:1, one launch (start us, length us, event | category | flops | bytes accessed | tf_op | source)
XLA Modules:
  0.0 493.1 jit_solution(4682429289840729518)
XLA Ops:
  7.2 1.6 copy.197
  10.8 15.7 %all-to-all-start = ((bf16[2,128,16]{1,0,2:T(2,128)(2,1)}), bf16[2,128,16]{1,0,2:T(2,128)(2,1)S(1)}, u32[]{:S(2)}, u32[]{:S(2)}) async-start(bf16[2,128,16]{1,0,2:T(2,128)(2,1)} %pad_maximum_fusion.3), calls=%async_computation | async-start | bytes 16384 | tf_op jit(solution)/shard_map/all_to_all | solution.py:424
  26.5 1.3 copy.143
  27.9 1.1 copy.165
  29.6 10.8 %copy.144 = bf16[3,128,2048]{1,0,2:T(4,128)(2,1)} copy(bf16[3,128,2048]{1,2,0:T(8,128)(2,1)S(1)} %pad_maximum_fusion) | data formatting | bytes 3145728 | tf_op jit(solution)/shard_map/stack | solution.py:420
  40.3 11.6 %all-to-all-start.1 = ((bf16[3,128,2048]{1,0,2:T(4,128)(2,1)}), bf16[3,128,2048]{1,0,2:T(4,128)(2,1)S(1)}, u32[]{:S(2)}, u32[]{:S(2)}) async-start(bf16[3,128,2048]{1,0,2:T(4,128)(2,1)} %copy.144), calls=%async_computation.1 | async-start | bytes 4194304 | tf_op jit(solution)/shard_map/all_to_all | solution.py:423
  56.1 105.9 %all-gather = f32[128,128]{1,0:T(8,128)S(1)} all-gather(f32[8,128]{1,0:T(8,128)S(1)} %pad_maximum_fusion.4), channel_id=2, replica_groups=mesh['segment'=16,'expert'=32] {'segment'}, dimensions={0}, use_global_device_ids=true | all-gather | bytes 69632 | tf_op jit(solution)/shard_map/all_gather | solution.py:358
  163.6 1.3 copy-done.1
  164.9 3.0 copy.146
  168.5 2.6 fusion.11
  171.1 1.2 convert_multiply_fusion.4
  172.3 1.1 fusion.74
  173.4 1.1 fusion.75
  174.6 1.1 fusion.76
  175.8 1.3 convolution_add_fusion.6
  177.1 1.2 convolution_add_fusion.5
  178.2 1.1 fusion.77
  179.4 1.2 convolution_add_fusion.4
  180.6 1.1 fusion.78
  181.8 1.2 convolution_add_fusion.3
  182.9 1.1 fusion.79
  184.1 1.4 convolution_add_fusion.2
  185.5 1.2 convolution_add_fusion.1
  186.7 1.9 fusion.8
  188.6 3.5 convolution_bitcast_fusion.1
  192.2 3.4 fusion.10
  195.6 3.5 convolution_multiply_fusion
  199.9 18.2 %while.12 = (s32[]{:T(128)}, f32[1,128,128]{2,1,0:T(8,128)S(1)}, f32[16,1,128,128]{3,2,1,0:T(8,128)S(1)}, f32[16,1,128,128]{3,2,1,0:T(8,128)}, f32[16,1,128,128]{3,2,1,0:T(8,128)}, /*index=5*/s32[]{:T(128)}) while((s32[]{:T(128)}, f32[1,128,128]{2,1,0:T(8,128)S(1)}, f32[16,1,128,128]{3,2,1,0:T(8,128)S(1)}, f32[16,1,128,128]{3,2,1,0:T(8,128)}, ...), condition=%wide.region_7.8_spmd, body=%wide.region_6.7_spmd.sunk | while | flops 25182208 | bytes 525393 | solution.py:486
  199.9 1.1 fusion.111
  201.1 1.1 fusion.111
  202.2 1.1 fusion.111
  203.4 1.1 fusion.111
  204.5 1.1 fusion.111
  205.6 1.1 fusion.111
  207.9 1.1 fusion.111
  209.1 1.1 fusion.111
  210.2 1.1 fusion.111
  211.3 1.1 fusion.111
  212.5 1.1 fusion.111
  217.0 1.1 fusion.111
  218.1 2.8 fusion.13
  220.9 2.2 convolution_multiply_fusion.1
  223.1 1.9 multiply_reduce_fusion
  226.3 10.8 %all-to-all-start.2 = ((bf16[16,128,128]{2,1,0:T(8,128)(2,1)}), bf16[16,128,128]{2,1,0:T(8,128)(2,1)S(1)}, u32[]{:S(2)}, u32[]{:S(2)}) async-start(bf16[16,128,128]{2,1,0:T(8,128)(2,1)} %copy.153), calls=%async_computation.2 | async-start | bytes 1048576 | tf_op jit(solution)/shard_map/all_to_all | solution.py:504
  241.3 1.1 pad_maximum_fusion.1.mix_ref
  243.0 12.9 %all-to-all-done.2 = bf16[16,128,128]{2,1,0:T(8,128)(2,1)S(1)} async-done(((bf16[16,128,128]{2,1,0:T(8,128)(2,1)}), bf16[16,128,128]{2,1,0:T(8,128)(2,1)S(1)}, u32[]{:S(2)}, u32[]{:S(2)}) %all-to-all-start.2) | async-done | bytes 524320 | tf_op jit(solution)/shard_map/all_to_all | solution.py:504
  257.3 226.6 %shard_map.158 = bf16[128,2048]{1,0:T(8,128)(2,1)} custom-call(s32[8,32,4]{2,1,0:T(8,128)} %copy.159.idx_ref, bf16[128,16,128]{2,1,0:T(8,128)(2,1)} %bitcast.193, bf16[128,2048]{1,0:T(8,128)(2,1)} %bitcast.195, bf16[8,2,128,256]{3,2,1,0:T(8,128)(2,1)} %pad_maximum_fusion.1.mix_ref, bf16[2048,256]{1,0:T(8,128)(2,1)} %bitcast.202, ...), custom_call_target="tpu_custom_call" | custom-call | tf_op jit(solution)/shard_map/pallas_call | solution.py:313
  483.9 1.9 copy.199
  (119 shorter events, 18.0 us)
Async XLA Ops:
  7.2 21.8 %copy-start.4 = (bf16[1,128,1024]{2,1,0:T(8,128)(2,1)S(1)}, bf16[1,128,1024]{2,1,0:T(8,128)(2,1)}, u32[]{:S(2)}) copy-start(bf16[1,128,1024]{2,1,0:T(8,128)(2,1)} %param.17) | copy-start | bytes 786436
  10.8 29.5 %all-to-all-start = ((bf16[2,128,16]{1,0,2:T(2,128)(2,1)}), bf16[2,128,16]{1,0,2:T(2,128)(2,1)S(1)}, u32[]{:S(2)}, u32[]{:S(2)}) async-start(bf16[2,128,16]{1,0,2:T(2,128)(2,1)} %pad_maximum_fusion.3), calls=%async_computation | async-start | bytes 16384 | tf_op jit(solution)/shard_map/all_to_all | solution.py:424
  40.3 12.4 %copy-start.8 = (s32[32]{0:T(128)S(1)}, s32[32]{0:T(128)}, u32[]{:S(2)}) copy-start(s32[32]{0:T(128)} %param.25) | copy-start | bytes 388
  40.3 15.8 %copy-start.5 = (s32[1,128,4]{1,2,0:T(4,128)S(1)}, s32[1,128,4]{1,2,0:T(4,128)}, u32[]{:S(2)}) copy-start(s32[1,128,4]{1,2,0:T(4,128)} %param.27) | copy-start | bytes 6148
  40.3 15.8 %copy-start.6 = (f32[1,128,4]{1,2,0:T(4,128)S(1)}, f32[1,128,4]{1,2,0:T(4,128)}, u32[]{:S(2)}) copy-start(f32[1,128,4]{1,2,0:T(4,128)} %param.28) | copy-start | bytes 6148
  40.3 123.2 %all-to-all-start.1 = ((bf16[3,128,2048]{1,0,2:T(4,128)(2,1)}), bf16[3,128,2048]{1,0,2:T(4,128)(2,1)S(1)}, u32[]{:S(2)}, u32[]{:S(2)}) async-start(bf16[3,128,2048]{1,0,2:T(4,128)(2,1)} %copy.144), calls=%async_computation.1 | async-start | bytes 4194304 | tf_op jit(solution)/shard_map/all_to_all | solution.py:423
  52.0 147.2 %all-gather.3.cloned.1.call-start = ((), (), s32[]{:S(2)}) async-start(), calls=%async_computation.3 | async-start | bytes 4325376 | tf_op jit(solution)/shard_map/all_gather | solution.py:430
  163.5 1.3 copy-start.1
  188.6 7.0 %copy-start = (f32[1,16,128,256]{3,2,1,0:T(8,128)}, f32[1,16,128,256]{3,2,1,0:T(8,128)S(1)}, u32[]{:S(2)}) copy-start(f32[1,16,128,256]{3,2,1,0:T(8,128)S(1)} %fusion.8) | copy-start | bytes 6291460
  220.9 2.2 copy-start.3
  223.1 2.0 copy-start.7
  226.3 29.6 %all-to-all-start.2 = ((bf16[16,128,128]{2,1,0:T(8,128)(2,1)}), bf16[16,128,128]{2,1,0:T(8,128)(2,1)S(1)}, u32[]{:S(2)}, u32[]{:S(2)}) async-start(bf16[16,128,128]{2,1,0:T(8,128)(2,1)} %copy.153), calls=%async_computation.2 | async-start | bytes 1048576 | tf_op jit(solution)/shard_map/all_to_all | solution.py:504
  256.3 1.0 copy-start.2
Sparse Core Ops, SparseCore 0:
  56.5 63.9 all-gather.2

commit v2 on v1

--- a/solution.py
+++ b/solution.py
@@ -5,28 +5,341 @@
 from jax.experimental.pallas import tpu as pltpu
 from jax.sharding import PartitionSpec as P
 
-BLOCK = 128
 MESH = pl.DeviceIdType.MESH
+
+
+def halves(block):
+    high = block.astype(jnp.bfloat16)
+    low = (block - high.astype(jnp.float32)).astype(jnp.bfloat16)
+    return high, low
+
+
+def left_pair(block):
+    high, low = halves(block)
+    return jnp.concatenate([high, low], axis=1)
+
+
+def right_pair(block):
+    high, low = halves(block)
+    row = jnp.concatenate([high, low], axis=1)
+    return jnp.concatenate([row, row], axis=0)
+
+
+def paired_dot(left, right):
+    both = jnp.dot(left, right, preferred_element_type=jnp.float32)
+    width = both.shape[1] // 2
+    return both[:, :width] + both[:, width:]
 
 
 def unit_rows(block, factor):
     squares = jnp.sum(block * block, axis=-1, keepdims=True)
-    return block * lax.rsqrt(squares + 1e-06) * factor
-
-
-def by_blocks(block, nblocks):
-    return block.reshape(nblocks, BLOCK, block.shape[1], block.shape[2]).transpose(2, 0, 1, 3)
-
-
-def unit_lower_inverse(lower_part, precise):
-    nilpotent = -lower_part
-    identity = jnp.eye(BLOCK, dtype=jnp.float32)
-    inverse = identity + nilpotent
-    power = nilpotent
-    for level in range(BLOCK.bit_length() - 2):
-        power = jnp.einsum("hnts,hnsu->hntu", power, power, precision=precise)
-        inverse = inverse + jnp.einsum("hnts,hnsu->hntu", inverse, power, precision=precise)
-    return inverse
+    return block * (lax.rsqrt(squares + 1e-06) * factor)
+
+
+def delta_kernel(
+    len_ref,
+    row_ref,
+    q_ref,
+    k_ref,
+    v_ref,
+    beta_ref,
+    decay_ref,
+    gain_ref,
+    store_ref,
+    mixed_ref,
+    rows_ref,
+    final_ref,
+    offer,
+    taken,
+    origin,
+    held,
+    passed,
+    step_left,
+    step_add,
+    ends,
+    tall,
+    strength_ref,
+    total_ref,
+    across_ref,
+    offer_send,
+    taken_recv,
+    origin_send,
+    held_recv,
+    passed_send,
+    ends_send,
+    final_recv,
+):
+    segments = lax.axis_size("segment")
+    columns = lax.axis_size("expert")
+    seg = lax.axis_index("segment")
+    col = lax.axis_index("expert")
+    tok = q_ref.shape[0]
+    dim = store_ref.shape[-1]
+    cached = store_ref.shape[0]
+    heads = segments
+    share = v_ref.shape[1] // q_ref.shape[1]
+
+    barrier = pltpu.get_barrier_semaphore()
+
+    def greet_row(step, carry):
+        other = lax.rem(col + step, columns)
+        pl.semaphore_signal(barrier, inc=1, device_id=(seg, other), device_id_type=MESH)
+        return carry
+
+    def greet_line(step, carry):
+        other = lax.rem(seg + step, segments)
+        pl.semaphore_signal(barrier, inc=1, device_id=(other, col), device_id_type=MESH)
+        return carry
+
+    lax.fori_loop(1, columns, greet_row, 0)
+    lax.fori_loop(1, segments, greet_line, 0)
+    pl.semaphore_wait(barrier, columns + segments - 2)
+
+    def propose(i, carry):
+        other = lax.rem(col + i, columns)
+        wanted = row_ref[other]
+        block = jnp.zeros((dim, dim), jnp.float32)
+        for r in range(cached):
+            match = jnp.where(wanted == col * cached + r, 1.0, 0.0)
+            block = block + store_ref[r, 0].astype(jnp.float32) * match
+        offer[other] = block.astype(jnp.bfloat16)
+
+        @pl.when(i == 0)
+        def _():
+            pltpu.make_async_copy(offer.at[col], taken.at[col], taken_recv).start()
+
+        @pl.when(i > 0)
+        def _():
+            pltpu.make_async_remote_copy(
+                src_ref=offer.at[other],
+                dst_ref=taken.at[col],
+                send_sem=offer_send,
+                recv_sem=taken_recv,
+                device_id=(seg, other),
+                device_id_type=MESH,
+            ).start()
+
+        return carry
+
+    lax.fori_loop(0, columns, propose, 0)
+
+    line = lax.broadcasted_iota(jnp.int32, (tok, tok), 0)
+    lane = lax.broadcasted_iota(jnp.int32, (tok, tok), 1)
+    place = lax.broadcasted_iota(jnp.int32, (tok, 1), 0)
+    valid = jnp.where(place + seg * tok < len_ref[0], 1.0, 0.0)
+    strength_ref[...] = beta_ref[...].astype(jnp.float32) * valid
+    logs = (decay_ref[...].astype(jnp.float32) * valid).astype(jnp.bfloat16)
+    lower = jnp.where(line >= lane, 1.0, 0.0).astype(jnp.bfloat16)
+    upper = jnp.where(line <= lane, 1.0, 0.0).astype(jnp.bfloat16)
+    total_ref[...] = jnp.dot(lower, logs, preferred_element_type=jnp.float32)
+    across_ref[...] = lax.dot_general(
+        logs, upper, (((0,), (0,)), ((), ())), preferred_element_type=jnp.float32
+    )
+    identity = jnp.where(line == lane, 1.0, 0.0)
+    which = lax.broadcasted_iota(jnp.int32, (tok, heads), 1)
+
+    def column_of(ref, j):
+        return jnp.sum(jnp.where(which == j, ref[...], 0.0), axis=1, keepdims=True)
+
+    def local_work(i, carry):
+        spot = pl.ds(pl.multiple_of(i * dim, dim), dim)
+        keys = unit_rows(k_ref[:, spot].astype(jnp.float32), 1.0)
+        queries = unit_rows(q_ref[:, spot].astype(jnp.float32), dim ** (-0.5))
+        keys_across = keys.T
+        grams = paired_dot(
+            left_pair(jnp.concatenate([keys, queries], axis=0)), right_pair(keys_across)
+        )
+        for a in range(share):
+            j = i * share + a
+            strength = column_of(strength_ref, j)
+            total = column_of(total_ref, j)
+            across = across_ref[pl.ds(j, 1), :]
+            last = across[:, tok - 1 :]
+            values = v_ref[:, pl.ds(pl.multiple_of(j * dim, dim), dim)].astype(jnp.float32)
+            spread = total - across
+            upto = jnp.where(line >= lane, jnp.exp(jnp.where(line >= lane, spread, 0.0)), 0.0)
+            coupling = jnp.where(line > lane, strength * upto * grams[:tok], 0.0)
+            inverse = identity - jnp.where((line == lane + 1) & (line % 2 == 1), coupling, 0.0)
+            size = 2
+            while size < tok:
+                corner = (
+                    (line // (2 * size) == lane // (2 * size))
+                    & ((line // size) % 2 == 1)
+                    & ((lane // size) % 2 == 0)
+                )
+                inner = paired_dot(
+                    left_pair(jnp.where(corner, coupling, 0.0)), right_pair(inverse)
+                )
+                inverse = inverse - paired_dot(left_pair(inverse), right_pair(inner))
+                size *= 2
+            growth = jnp.exp(total)
+            solver = left_pair(inverse)
+            pseudo = right_pair(paired_dot(solver, right_pair(strength * values)))
+            weights = right_pair(paired_dot(solver, right_pair((strength * growth) * keys)))
+            tail = keys_across * jnp.exp(last - across)
+            scores = upto * grams[tok:]
+            left = left_pair(jnp.concatenate([tail, scores], axis=0))
+            minus = paired_dot(left, weights)
+            step_add[j] = paired_dot(left, pseudo)
+            step_left[j] = left_pair(
+                jnp.concatenate([jnp.exp(last) * identity, growth * queries], axis=0) - minus
+            )
+        return carry
+
+    def hand_on(j, carry):
+        return pltpu.make_async_remote_copy(
+            src_ref=passed.at[j],
+            dst_ref=held.at[j],
+            send_sem=passed_send.at[j],
+            recv_sem=held_recv.at[j],
+            device_id=(seg + 1, col),
+            device_id_type=MESH,
+        )
+
+    def origin_copy():
+        return pltpu.make_async_remote_copy(
+            src_ref=origin,
+            dst_ref=held.at[seg],
+            send_sem=origin_send,
+            recv_sem=held_recv.at[seg],
+            device_id=(0, col),
+            device_id_type=MESH,
+        )
+
+    def end_copy(j):
+        return pltpu.make_async_remote_copy(
+            src_ref=ends.at[j],
+            dst_ref=final_ref,
+            send_sem=ends_send.at[j],
+            recv_sem=final_recv,
+            device_id=(j, col),
+            device_id_type=MESH,
+        )
+
+    def give_origin():
+        pltpu.make_async_copy(taken, taken, taken_recv).wait()
+
+        def add_up(i, block):
+            return block + taken[i].astype(jnp.float32)
+
+        origin[...] = lax.fori_loop(0, columns, add_up, jnp.zeros((dim, dim), jnp.float32))
+
+        @pl.when(seg == 0)
+        def _():
+            pltpu.make_async_copy(origin, held.at[0], held_recv.at[0]).start()
+
+        @pl.when(seg > 0)
+        def _():
+            origin_copy().start()
+
+    def local_step(i, carry):
+        local_work(i, carry)
+
+        @pl.when(i == heads // share // 2)
+        def _():
+            give_origin()
+
+        return carry
+
+    lax.fori_loop(0, heads // share, local_step, 0)
+
+    def chain(j, carry):
+        pltpu.make_async_copy(held.at[j], held.at[j], held_recv.at[j]).wait()
+        state = right_pair(held[j])
+        passed[j] = paired_dot(step_left[j, :dim], state) + step_add[j, :dim]
+
+        @pl.when(seg < segments - 1)
+        def _():
+            hand_on(j, 0).start()
+
+        @pl.when(seg == segments - 1)
+        def _():
+            ends[j] = passed[j].astype(jnp.bfloat16)
+
+            @pl.when(j < segments - 1)
+            def _():
+                end_copy(j).start()
+
+            @pl.when(j == segments - 1)
+            def _():
+                pltpu.make_async_copy(ends.at[j], final_ref, final_recv).start()
+
+        raw = (paired_dot(step_left[j, dim:], state) + step_add[j, dim:]) * valid
+        squares = jnp.sum(raw * raw, axis=-1, keepdims=True) * (1.0 / dim)
+        normed = raw * lax.rsqrt(squares + 1e-06) * gain_ref[...]
+        mixed_ref[:, pl.ds(pl.multiple_of(j * dim, dim), dim)] = normed.astype(jnp.bfloat16)
+        tall[pl.ds(j, tok, stride=heads), :] = normed
+        return carry
+
+    lax.fori_loop(0, heads, chain, 0)
+    rows_ref[...] = tall[...].astype(jnp.bfloat16).reshape(tok, heads, dim)
+    pltpu.make_async_copy(final_ref, final_ref, final_recv).wait()
+
+    sent = offer.at[pl.ds(0, columns - 1)]
+    pltpu.make_async_copy(sent, sent, offer_send).wait()
+
+    @pl.when(seg > 0)
+    def _():
+        origin_copy().wait_send()
+
+    def drain(j, carry):
+        @pl.when(seg < segments - 1)
+        def _():
+            hand_on(j, 0).wait_send()
+
+        @pl.when((seg == segments - 1) & (j < segments - 1))
+        def _():
+            end_copy(j).wait_send()
+
+        return carry
+
+    lax.fori_loop(0, heads, drain, 0)
+
+
+def delta(suffix_len, cache_row, q, k, v, beta, decay, gain, store):
+    segments = lax.axis_size("segment")
+    columns = lax.axis_size("expert")
+    tok, width = v.shape
+    dim = store.shape[-1]
+    heads = segments
+    bf, f32 = jnp.bfloat16, jnp.float32
+    dma = pltpu.SemaphoreType.DMA
+    whole = pl.BlockSpec(memory_space=pltpu.VMEM)
+    scalars = pl.BlockSpec(memory_space=pltpu.SMEM)
+    return pl.pallas_call(
+        delta_kernel,
+        out_shape=(
+            jax.ShapeDtypeStruct((tok, width), bf),
+            jax.ShapeDtypeStruct((tok, heads, dim), bf),
+            jax.ShapeDtypeStruct((dim, dim), bf),
+        ),
+        in_specs=[scalars, scalars] + [whole] * 7,
+        out_specs=(whole, whole, whole),
+        scratch_shapes=[
+            pltpu.VMEM((columns, dim, dim), bf),
+            pltpu.VMEM((columns, dim, dim), bf),
+            pltpu.VMEM((dim, dim), f32),
+            pltpu.VMEM((heads, dim, dim), f32),
+            pltpu.VMEM((heads, dim, dim), f32),
+            pltpu.VMEM((heads, 2 * dim, 2 * dim), bf),
+            pltpu.VMEM((heads, 2 * dim, dim), f32),
+            pltpu.VMEM((heads, dim, dim), bf),
+            pltpu.VMEM((tok * heads, dim), f32),
+            pltpu.VMEM((tok, heads), f32),
+            pltpu.VMEM((tok, heads), f32),
+            pltpu.VMEM((heads, tok), f32),
+            dma,
+            dma,
+            dma,
+            dma((heads,)),
+            dma((heads,)),
+            dma((heads,)),
+            dma,
+        ],
+        compiler_params=pltpu.CompilerParams(
+            collective_id=2, has_side_effects=True, vmem_limit_bytes=40 * 1024 * 1024
+        ),
+    )(suffix_len, cache_row, q, k, v, beta, decay, gain, store)
 
 
 def moe_kernel(
@@ -403,107 +716,19 @@
     w_up,
     w_down,
 ):
-    precise = lax.Precision.HIGHEST
-    segments = lax.axis_size("segment")
-    columns = lax.axis_size("expert")
-    column = lax.axis_index("expert")
-    tok_dev = q_heads.shape[1]
-    heads_here = store_states.shape[1]
-    key_dim = store_states.shape[2]
-    head_total = values.shape[2] // key_dim
-    repeat_count = head_total // (q_heads.shape[2] // key_dim)
-
-    def widen(block):
-        shaped = block[0].reshape(tok_dev, -1, key_dim)
-        return jnp.repeat(shaped, repeat_count, axis=1).reshape(tok_dev, head_total * key_dim)
-
-    packed = jnp.stack([widen(q_heads), widen(k_heads), values[0]])
-    gating = jnp.stack([beta[0], decay[0]])
-    packed, gating = (
-        lax.all_to_all(packed, "segment", split_axis=2, concat_axis=1, tiled=True),
-        lax.all_to_all(gating, "segment", split_axis=2, concat_axis=1, tiled=True),
+    mixed, rows, final = delta(
+        suffix_len,
+        cache_row,
+        q_heads[0],
+        k_heads[0],
+        values[0],
+        beta[0],
+        decay[0],
+        head_gain.reshape(1, -1),
+        store_states,
     )
-    suffix = packed.shape[1]
-    nblocks = suffix // BLOCK
-    my_row = cache_row[column]
-    empty_state = jnp.zeros(store_states.shape[1:], jnp.bfloat16)
-    piece = lax.all_gather(store_states, "expert", axis=0, tiled=True)
-    inside = (my_row >= 0) & (my_row < piece.shape[0])
-    taken = lax.dynamic_index_in_dim(
-        piece, jnp.clip(my_row, 0, piece.shape[0] - 1), 0, keepdims=False
-    )
-    initial = jnp.where(inside, taken, empty_state)
-    queries = by_blocks(
-        unit_rows(
-            packed[0].astype(jnp.float32).reshape(suffix, heads_here, key_dim), key_dim ** (-0.5)
-        ),
-        nblocks,
-    )
-    keys_unit = by_blocks(
-        unit_rows(packed[1].astype(jnp.float32).reshape(suffix, heads_here, key_dim), 1.0), nblocks
-    )
-    values_f = by_blocks(
-        packed[2].astype(jnp.float32).reshape(suffix, heads_here, key_dim), nblocks
-    )
-    valid = (jnp.arange(suffix, dtype=jnp.int32) < suffix_len[0]).astype(jnp.float32)
-    strength = (
-        (gating[0].astype(jnp.float32) * valid[:, None])
-        .reshape(nblocks, BLOCK, heads_here)
-        .transpose(2, 0, 1)
-    )
-    log_decay = (
-        (gating[1].astype(jnp.float32) * valid[:, None])
-        .reshape(nblocks, BLOCK, heads_here)
-        .transpose(2, 0, 1)
-    )
-    cumulative = jnp.cumsum(log_decay, axis=-1)
-    spread = cumulative[..., :, None] - cumulative[..., None, :]
-    strict = jnp.tril(jnp.ones((BLOCK, BLOCK), bool), -1)
-    inclusive = jnp.tril(jnp.ones((BLOCK, BLOCK), bool), 0)
-    below = jnp.where(strict, jnp.exp(jnp.where(strict, spread, 0.0)), 0.0)
-    upto = jnp.where(inclusive, jnp.exp(jnp.where(inclusive, spread, 0.0)), 0.0)
-    key_gram = jnp.einsum("hnti,hnsi->hnts", keys_unit, keys_unit, precision=precise)
-    lower_part = strength[..., None] * below * key_gram
-    growth = jnp.exp(cumulative)
-    targets = jnp.concatenate(
-        [strength[..., None] * values_f, (strength * growth)[..., None] * keys_unit], axis=-1
-    )
-    inverse = unit_lower_inverse(lower_part, precise)
-    solved = jnp.einsum("hnts,hnsj->hntj", inverse, targets, precision=precise)
-    pseudo = solved[..., :key_dim]
-    weights_wy = solved[..., key_dim:]
-    tail_decay = jnp.exp(cumulative[..., -1:] - cumulative)
-    keys_tail = keys_unit * tail_decay[..., None]
-    transition = growth[..., -1][..., None, None] * jnp.eye(
-        key_dim, dtype=jnp.float32
-    ) - jnp.einsum("hnti,hntj->hnij", keys_tail, weights_wy, precision=precise)
-    injection = jnp.einsum("hnti,hntj->hnij", keys_tail, pseudo, precision=precise)
-
-    def advance(state, inputs):
-        matrix, offset = inputs
-        return (jnp.einsum("hij,hjk->hik", matrix, state, precision=precise) + offset, state)
-
-    final_state, starts = lax.scan(
-        advance,
-        initial.astype(jnp.float32),
-        (jnp.moveaxis(transition, 1, 0), jnp.moveaxis(injection, 1, 0)),
-    )
-    starts = jnp.moveaxis(starts, 0, 1)
-    corrected = pseudo - jnp.einsum("hnti,hnij->hntj", weights_wy, starts, precision=precise)
-    scores = upto * jnp.einsum("hnti,hnsi->hnts", queries, keys_unit, precision=precise)
-    raw = growth[..., None] * jnp.einsum("hnti,hnij->hntj", queries, starts, precision=precise)
-    raw = raw + jnp.einsum("hnts,hnsj->hntj", scores, corrected, precision=precise)
-    raw = raw * valid.reshape(nblocks, BLOCK)[None, :, :, None]
-    normed = raw * lax.rsqrt(jnp.mean(raw * raw, axis=-1, keepdims=True) + 1e-06) * head_gain
-    mixed_heads = (
-        normed.transpose(1, 2, 0, 3).reshape(suffix, heads_here * key_dim).astype(jnp.bfloat16)
-    )
-    store_out = lax.dynamic_update_index_in_dim(
-        store_states, final_state.astype(jnp.bfloat16), write_slot[0], 0
-    )
-    mixed = lax.all_to_all(mixed_heads, "segment", split_axis=0, concat_axis=1, tiled=True)
     index, mix = route_tables(expert_ids[0], route_weight[0])
-    rows = mixed.reshape(tok_dev, head_total, key_dim)
+    store_out = lax.dynamic_update_index_in_dim(store_states, final[None], write_slot[0], 0)
     out = moe(index, rows, mixed, mix, w_gate[0], w_up[0], w_down[0])
     return (out[None], store_out)
 

time: 502 us -> 394 us (0.78); the launches traced: 493 us -> 393 us
  Pallas kernels: 227 us -> 349 us
  blocking collectives: 106 us -> 29.6 us
  matrix products: 53.6 us -> 0 us
  starting transfers between devices: 38.2 us -> 0 us
  local copies, waits for them, and re-layouts: 28.8 us -> 8.69 us
  between operations: 18.3 us -> 2.17 us
  waiting for transfers between devices: 13.6 us -> 0 us
    pallas_call x0 -> x1, Pallas kernels: none -> 101 us  [delta(): pl.pallas_call(delta_kernel, out_shape=(jax.ShapeDtypeStruct((tok, width)...]
    all_gather x1, blocking collectives: 106 us -> 29.6 us  [route_tables(): routes = lax.all_gather(routes, 'segment', axis=0, tiled=False)]
    dot_general x36 -> x0, matrix products: 53.6 us -> none  [the longest x16 17.3 us: advance(): jnp.einsum('hij,hjk->hik', matrix, state, precision=precise) + offset]
    all_to_all x3 -> x0, starting transfers between devices: 38.2 us -> none  [the longest x1 15.7 us: shards(): lax.all_to_all(gating, 'segment', split_axis=2, concat_axis=1, tiled=True)]
    pallas_call x1, Pallas kernels: 227 us -> 248 us  [moe(): pl.pallas_call(moe_kernel, out_shape=jax.ShapeDtypeStruct((tok, width), b...]
    all_to_all x3 -> x0, waiting for transfers between devices: 12.9 us -> none  [the longest x1 12.9 us: shards(): lax.all_to_all(mixed_heads, 'segment', split_axis=0, concat_axis=1, tiled...]
    another operation x3 -> x0, local copies, waits for them, and re-layouts: 12 us -> none  [the longest x1 10.8 us: shards(): packed = jnp.stack([widen(q_heads), widen(k_heads), values[0]])]
  transfers between devices with their start and end apart: 4 -> 0, of which waited for: 1 -> 0; matrix products, arithmetic and copies ran while one was open for 11% -> 0% of each run, Pallas kernels for 0% -> 0%
where the time goes in v2:
time: 394 us; the launch traced here: 393 us
  Pallas kernels  349 us (89%)
  blocking collectives  29.6 us (8%)
  local copies, waits for them, and re-layouts  8.69 us (2%)
  other arithmetic  4.06 us (1%)
    pallas_call x1, Pallas kernels, moe(): pl.pallas_call(moe_kernel, out_shape=jax.ShapeDtypeStruct((tok, width), b...  248 us
    pallas_call x1, Pallas kernels, delta(): pl.pallas_call(delta_kernel, out_shape=(jax.ShapeDtypeStruct((tok, width)...  101 us
    all_gather x1, blocking collectives, route_tables(): routes = lax.all_gather(routes, 'segment', axis=0, tiled=False)  29.6 us

profile of v2, /device:TPU:1, one launch (start us, length us, event | category | flops | bytes accessed | tf_op | source)
XLA Modules:
  0.0 393.3 jit_solution(9984973458933617708)
XLA Ops:
  0.6 0.9 copy.67.store_ref
  2.9 0.7 convert_bitcast_fusion
  3.6 0.7 pad_maximum_fusion.2
  4.3 0.1 copy.46
  4.3 0.1 reshape.210
  4.4 0.8 copy.50
  5.2 0.8 copy.51
  6.0 29.6 %all-gather = f32[128,128]{1,0:T(8,128)S(1)} all-gather(f32[8,128]{1,0:T(8,128)S(1)} %pad_maximum_fusion.2), channel_id=2, replica_groups=mesh['segment'=16,'expert'=32] {'segment'}, dimensions={0}, use_global_device_ids=true | all-gather | bytes 69632 | tf_op jit(solution)/shard_map/all_gather | solution.py:671
  35.6 0.6 gather_fusion
  36.2 0.2 compare_reduce_fusion
  36.4 0.6 select_reduce_fusion.1
  37.1 0.8 copy.56.idx_ref
  37.9 0.2 fusion
  38.1 0.3 bitcast_select_fusion.1
  38.4 0.2 copy.57
  38.6 0.1 concatenate.34.clone
  38.6 0.2 copy.54
  38.9 0.2 copy.58
  39.1 0.1 concatenate.35.clone
  39.1 0.2 copy.55
  39.3 0.2 reduce-precision_convert_fusion
  39.5 0.0 copy-start.2
  39.6 0.0 copy-start.4
  39.6 0.0 copy-start.5
  39.6 0.0 copy-start.6
  39.6 0.0 copy-start.7
  39.6 1.1 pad_maximum_fusion.mix_ref
  40.7 0.0 copy-done.2
  40.7 0.0 copy-done.4
  40.7 0.3 copy-done.5
  41.0 0.0 copy-done.6
  41.0 0.0 copy-done.7
  41.0 101.3 %shard_map.158 = (bf16[128,2048]{1,0:T(8,128)(2,1)S(1)}, bf16[128,16,128]{2,1,0:T(8,128)(2,1)S(1)}, bf16[128,128]{1,0:T(8,128)(2,1)S(1)}) custom-call(s32[1]{0:T(128)S(6)} %copy.65.len_ref, s32[32]{0:T(128)S(1)} %copy-done.6, bf16[128,1024]{1,0:T(8,128)(2,1)S(1)} %bitcast.54, bf16[128,1024]{1,0:T(8,128)(2,1)S(1)} %bitcast.55, ...), custom_call_target="tpu_custom_call" | custom-call | tf_op jit(solution)/shard_map/pallas_call | solution.py:309
  142.3 0.0 copy-start
  142.3 0.8 copy-done
  143.1 0.0 copy-start.1
  143.1 0.8 copy-done.1
  143.9 0.0 copy-start.3
  143.9 247.5 %shard_map.159 = bf16[128,2048]{1,0:T(8,128)(2,1)} custom-call(s32[8,32,4]{2,1,0:T(8,128)} %copy.56.idx_ref, bf16[128,16,128]{2,1,0:T(8,128)(2,1)} %copy-done.1, bf16[128,2048]{1,0:T(8,128)(2,1)} %copy-done, bf16[8,2,128,256]{3,2,1,0:T(8,128)(2,1)} %pad_maximum_fusion.mix_ref, bf16[2048,256]{1,0:T(8,128)(2,1)} %bitcast.62, bf16[2048,256]{1,0:T(8,128)(2,1)} %bitcast.63, ...), custom_call_target="tpu_custom_call" | custom-call | tf_op jit(solution)/shard_map/pallas_call | solution.py:626
  391.5 0.0 copy-done.3
  391.5 1.9 copy.68
  (13 shorter events, 0.1 us)
Async XLA Ops:
  39.5 1.2 copy-start.2
  39.6 1.2 copy-start.4
  39.6 1.4 copy-start.5
  39.6 1.4 copy-start.6
  39.6 1.4 copy-start.7
  142.3 0.8 copy-start
  143.1 0.8 copy-start.1
  143.9 247.5 %copy-start.3 = (bf16[4,1,128,128]{3,2,1,0:T(8,128)(2,1)}, bf16[4,1,128,128]{3,2,1,0:T(8,128)(2,1)S(1)}, u32[]{:S(2)}) copy-start(bf16[4,1,128,128]{3,2,1,0:T(8,128)(2,1)S(1)} %bitcast_dynamic-update-slice_fusion) | copy-start | bytes 393220

commit v3 on v2

v3 whole, which is shorter than its diff:
```python
import jax
import jax.numpy as jnp
from jax import lax
from jax.experimental import pallas as pl
from jax.experimental.pallas import tpu as pltpu
from jax.sharding import PartitionSpec as P

MESH = pl.DeviceIdType.MESH


GROUP = 4


def halves(block):
    high = block.astype(jnp.bfloat16)
    low = (block - high.astype(jnp.float32)).astype(jnp.bfloat16)
    return high, low


def left_pair(block):
    high, low = halves(block)
    return jnp.concatenate([high, low], axis=1)


def right_pair(block):
    high, low = halves(block)
    row = jnp.concatenate([high, low], axis=1)
    return jnp.concatenate([row, row], axis=0)


def paired_dot(left, right):
    both = jnp.dot(left, right, preferred_element_type=jnp.float32)
    width = both.shape[1] // 2
    return both[:, :width] + both[:, width:]


def unit_rows(block, factor):
    squares = jnp.sum(block * block, axis=-1, keepdims=True)
    return block * (lax.rsqrt(squares + 1e-06) * factor)


def mixer_kernel(
    len_ref,
    row_ref,
    slot_ref,
    beta_ref,
    decay_ref,
    gain_ref,
    ids_ref,
    weight_ref,
    store_in,
    k_in,
    q_in,
    v_in,
    gate_in,
    up_in,
    down_in,
    out_ref,
    store_out_ref,
    store_ref,
    k_ref,
    q_ref,
    v_ref,
    gate_ref,
    up_ref,
    down_ref,
    routes_ref,
    routes_all,
    index_ref,
    idx_ref,
    mix_ref,
    spread_ref,
    mixed_ref,
    rows_ref,
    final_ref,
    offer,
    taken,
    origin,
    held,
    passed,
    step_left,
    step_add,
    strength_ref,
    total_ref,
    across_ref,
    climb,
    sink,
    distant,
    pick,
    stage,
    arrive,
    back,
    flat,
    sum_up,
    sum_down,
    got_up,
    got_down,
    tall,
    wide,
    load_sem,
    routes_send,
    routes_recv,
    index_sem,
    offer_send,
    taken_recv,
    origin_send,
    held_recv,
    passed_send,
    ends_send,
    final_recv,
    distant_send,
    distant_recv,
    climb_send,
    climb_recv,
    sink_send,
    sink_recv,
    stage_send,
    arrive_recv,
    back_send,
    back_recv,
    up_send,
    up_recv,
    down_send,
    down_recv,
):
    segments = lax.axis_size("segment")
    columns = lax.axis_size("expert")
    seg = lax.axis_index("segment")
    col = lax.axis_index("expert")
    pairs = segments // 2
    tok = q_ref.shape[0]
    half = tok // 2
    dim = store_ref.shape[-1]
    cached = store_ref.shape[0]
    heads = segments
    share = v_ref.shape[1] // q_ref.shape[1]
    top = ids_ref.shape[0]
    above = lax.rem(seg + 1, segments)
    below = lax.rem(seg + segments - 1, segments)

    def load(source, target, k):
        return pltpu.make_async_copy(source, target, load_sem.at[k])

    for k, (source, target) in enumerate(
        (
            (store_in, store_ref),
            (k_in, k_ref),
            (q_in, q_ref),
            (v_in, v_ref),
            (gate_in, gate_ref),
            (up_in, up_ref),
            (down_in, down_ref),
        )
    ):
        load(source, target, k).start()
    routes_ref[:top] = ids_ref[...].astype(jnp.float32)
    routes_ref[top:] = weight_ref[...]

    barrier = pltpu.get_barrier_semaphore()

    def greet_row(step, carry):
        other = lax.rem(col + step, columns)
        pl.semaphore_signal(barrier, inc=1, device_id=(seg, other), device_id_type=MESH)
        return carry

    def greet_line(step, carry):
        other = lax.rem(seg + step, segments)
        pl.semaphore_signal(barrier, inc=1, device_id=(other, col), device_id_type=MESH)
        return carry

    lax.fori_loop(1, columns, greet_row, 0)
    lax.fori_loop(1, segments, greet_line, 0)
    pl.semaphore_wait(barrier, columns + segments - 2)

    far = segments // 2
    pltpu.make_async_copy(routes_ref, routes_all.at[0], routes_recv).start()

    def routes_copy(step, slot):
        return pltpu.make_async_remote_copy(
            src_ref=routes_ref,
            dst_ref=routes_all.at[slot],
            send_sem=routes_send.at[slot],
            recv_sem=routes_recv,
            device_id=(lax.rem(seg + step, segments), col),
            device_id_type=MESH,
        )

    def routes_out(k, carry):
        routes_copy(k, 2 * k - 1).start()
        routes_copy(segments - k, 2 * k).start()
        return carry

    lax.fori_loop(1, far, routes_out, 0)
    routes_copy(far, segments - 1).start()

    load(store_in, store_ref, 0).wait()

    def propose(i, carry):
        other = lax.rem(col + i, columns)
        wanted = row_ref[other]
        block = jnp.zeros((dim, dim), jnp.float32)
        for r in range(cached):
            match = jnp.where(wanted == col * cached + r, 1.0, 0.0)
            block = block + store_ref[r, 0].astype(jnp.float32) * match
        offer[other] = block.astype(jnp.bfloat16)

        @pl.when(i == 0)
        def _():
            pltpu.make_async_copy(offer.at[col], taken.at[col], taken_recv).start()

        @pl.when(i > 0)
        def _():
            pltpu.make_async_remote_copy(
                src_ref=offer.at[other],
                dst_ref=taken.at[col],
                send_sem=offer_send,
                recv_sem=taken_recv,
                device_id=(seg, other),
                device_id_type=MESH,
            ).start()

        return carry

    lax.fori_loop(0, columns, propose, 0)

    line = lax.broadcasted_iota(jnp.int32, (tok, tok), 0)
    lane = lax.broadcasted_iota(jnp.int32, (tok, tok), 1)
    place = lax.broadcasted_iota(jnp.int32, (tok, 1), 0)
    valid = jnp.where(place + seg * tok < len_ref[0], 1.0, 0.0)
    along = lax.broadcasted_iota(jnp.int32, (1, tok), 1)
    valid_along = jnp.where(along + seg * tok < len_ref[0], 1.0, 0.0)
    logs = (decay_ref[...].astype(jnp.float32) * valid_along).astype(jnp.bfloat16)
    writes = (beta_ref[...].astype(jnp.float32) * valid_along).astype(jnp.bfloat16)
    lower = jnp.where(line >= lane, 1.0, 0.0).astype(jnp.bfloat16)
    upper = jnp.where(line <= lane, 1.0, 0.0).astype(jnp.bfloat16)
    diagonal = jnp.where(line == lane, 1.0, 0.0).astype(jnp.bfloat16)
    turned = (((1,), (1,)), ((), ()))
    across_ref[...] = jnp.dot(logs, upper, preferred_element_type=jnp.float32)
    total_ref[...] = lax.dot_general(lower, logs, turned, preferred_element_type=jnp.float32)
    strength_ref[...] = lax.dot_general(
        diagonal, writes, turned, preferred_element_type=jnp.float32
    )
    for k, (source, target) in enumerate(((k_in, k_ref), (q_in, q_ref), (v_in, v_ref))):
        load(source, target, k + 1).wait()
    identity = jnp.where(line == lane, 1.0, 0.0)
    which = lax.broadcasted_iota(jnp.int32, (tok, heads), 1)

    def column_of(ref, j):
        return jnp.sum(jnp.where(which == j, ref[...], 0.0), axis=1, keepdims=True)

    def local_work(i, carry):
        grams, across_keys, unit_keys, unit_queries = [], [], [], []
        for g in range(GROUP):
            spot = pl.ds(pl.multiple_of((i * GROUP + g) * dim, dim), dim)
            keys = unit_rows(k_ref[:, spot].astype(jnp.float32), 1.0)
            queries = unit_rows(q_ref[:, spot].astype(jnp.float32), dim ** (-0.5))
            unit_keys.append(keys)
            unit_queries.append(queries)
            across_keys.append(keys.T)
        for g in range(GROUP):
            grams.append(
                paired_dot(
                    left_pair(jnp.concatenate([unit_keys[g], unit_queries[g]], axis=0)),
                    right_pair(across_keys[g]),
                )
            )
        count = GROUP * share
        number = [i * count + a for a in range(count)]
        strength = [column_of(strength_ref, j) for j in number]
        total = [column_of(total_ref, j) for j in number]
        across = [across_ref[pl.ds(j, 1), :] for j in number]
        upto = [
            jnp.where(line >= lane, jnp.exp(jnp.where(line >= lane, total[a] - across[a], 0.0)), 0.0)
            for a in range(count)
        ]
        coupling = [
            jnp.where(line > lane, strength[a] * upto[a] * grams[a // share][:tok], 0.0)
            for a in range(count)
        ]
        inverse = [
            identity - jnp.where((line == lane + 1) & (line % 2 == 1), coupling[a], 0.0)
            for a in range(count)
        ]
        size = 2
        while size < tok:
            corner = (
                (line // (2 * size) == lane // (2 * size))
                & ((line // size) % 2 == 1)
                & ((lane // size) % 2 == 0)
            )
            inner = [
                paired_dot(
                    left_pair(jnp.where(corner, coupling[a], 0.0)), right_pair(inverse[a])
                )
                for a in range(count)
            ]
            inverse = [
                inverse[a] - paired_dot(left_pair(inverse[a]), right_pair(inner[a]))
                for a in range(count)
            ]
            size *= 2
        growth = [jnp.exp(total[a]) for a in range(count)]
        solver = [left_pair(inverse[a]) for a in range(count)]
        pseudo = []
        for a in range(count):
            spot = pl.ds(pl.multiple_of(number[a] * dim, dim), dim)
            values = v_ref[:, spot].astype(jnp.float32)
            pseudo.append(right_pair(paired_dot(solver[a], right_pair(strength[a] * values))))
        weights = [
            right_pair(
                paired_dot(solver[a], right_pair((strength[a] * growth[a]) * unit_keys[a // share]))
            )
            for a in range(count)
        ]
        for a in range(count):
            last = across[a][:, tok - 1 :]
            tail = across_keys[a // share] * jnp.exp(last - across[a])
            scores = upto[a] * grams[a // share][tok:]
            left = left_pair(jnp.concatenate([tail, scores], axis=0))
            minus = paired_dot(left, weights[a])
            step_add[number[a]] = paired_dot(left, pseudo[a])
            step_left[number[a]] = left_pair(
                jnp.concatenate(
                    [jnp.exp(last) * identity, growth[a] * unit_queries[a // share]], axis=0
                )
                - minus
            )
        return carry

    def hand_on(j, carry):
        return pltpu.make_async_remote_copy(
            src_ref=passed.at[j],
            dst_ref=held.at[j],
            send_sem=passed_send.at[j],
            recv_sem=held_recv.at[j],
            device_id=(seg + 1, col),
            device_id_type=MESH,
        )

    def origin_copy():
        return pltpu.make_async_remote_copy(
            src_ref=origin,
            dst_ref=held.at[seg],
            send_sem=origin_send,
            recv_sem=held_recv.at[seg],
            device_id=(0, col),
            device_id_type=MESH,
        )

    def end_copy(j):
        return pltpu.make_async_remote_copy(
            src_ref=passed.at[j],
            dst_ref=final_ref,
            send_sem=ends_send.at[j],
            recv_sem=final_recv,
            device_id=(j, col),
            device_id_type=MESH,
        )

    def give_origin():
        pltpu.make_async_copy(taken, taken, taken_recv).wait()

        def add_up(i, block):
            return block + taken[i].astype(jnp.float32)

        block = lax.fori_loop(0, columns, add_up, jnp.zeros((dim, dim), jnp.float32))
        origin[:, :dim] = block.astype(jnp.bfloat16)
        origin[:, dim:] = jnp.zeros((dim, dim), jnp.bfloat16)

        @pl.when(seg == 0)
        def _():
            pltpu.make_async_copy(origin, held.at[0], held_recv.at[0]).start()

        @pl.when(seg > 0)
        def _():
            origin_copy().start()

    def local_step(i, carry):
        local_work(i, carry)

        @pl.when(i == heads // share // GROUP // 2)
        def _():
            give_origin()

        return carry

    lax.fori_loop(0, heads // share // GROUP, local_step, 0)

    names = lax.broadcasted_iota(jnp.int32, (columns, 1), 0) + seg * columns
    token = lax.broadcasted_iota(jnp.int32, (columns, tok), 1)

    def locate(slot):
        routes = routes_all[slot]
        top = routes.shape[0] // 2
        weight = jnp.zeros((columns, tok), jnp.float32)
        first = jnp.full((columns, tok), tok, jnp.int32)
        last = jnp.full((columns, tok), -1, jnp.int32)
        for k in range(top):
            same = routes[k : k + 1, :].astype(jnp.int32) == names
            weight = weight + jnp.where(same, routes[top + k : top + k + 1, :], 0.0)
            first = jnp.where(same, token, first)
            last = jnp.where(same, token, last)
        first = jnp.min(first, axis=1, keepdims=True)
        last = jnp.max(last, axis=1, keepdims=True)
        index_ref[slot] = jnp.where(token == 0, jnp.where(first < tok, first, 0), jnp.maximum(last, 0))
        pltpu.make_async_copy(index_ref.at[slot], idx_ref.at[slot], index_sem).start()
        at_first = jnp.where(token == first, weight, 0.0)
        at_last = jnp.where((token == last) & (last != first), weight, 0.0)
        return at_first, at_last

    def tabulate(slot, p, source, width):
        at_first, at_last = locate(slot)
        spread_ref[...] = jnp.zeros_like(spread_ref)
        spread_ref[pl.ds(2 * source, columns, stride=width), :] = at_first
        spread_ref[pl.ds(2 * source + 1, columns, stride=width), :] = at_last
        mix_ref[p, source] = left_pair(spread_ref[...].T)

    def chain(j, carry):
        pltpu.make_async_copy(held.at[j], held.at[j], held_recv.at[j]).wait()
        state = jnp.concatenate([held[j], held[j]], axis=0)
        passed[j] = left_pair(paired_dot(step_left[j, :dim], state) + step_add[j, :dim])

        @pl.when(seg < segments - 1)
        def _():
            hand_on(j, 0).start()

        @pl.when((seg == segments - 1) & (j < segments - 1))
        def _():
            end_copy(j).start()

        @pl.when((seg == segments - 1) & (j == segments - 1))
        def _():
            pltpu.make_async_copy(passed.at[j], final_ref, final_recv).start()

        raw = (paired_dot(step_left[j, dim:], state) + step_add[j, dim:]) * valid
        squares = jnp.sum(raw * raw, axis=-1, keepdims=True) * (1.0 / dim)
        normed = raw * lax.rsqrt(squares + 1e-06) * gain_ref[...]
        mixed_ref[:, pl.ds(pl.multiple_of(j * dim, dim), dim)] = normed.astype(jnp.bfloat16)
        tall[pl.ds(j, tok, stride=heads), :] = normed

        @pl.when(j == 0)
        def _():
            pltpu.make_async_copy(routes_all, routes_all, routes_recv).wait()
            tabulate(0, 0, 0, 4)
            tabulate(segments - 1, far, 0, 2)

        @pl.when((j > 0) & (j < far))
        def _():
            tabulate(2 * j - 1, j, 0, 4)
            tabulate(2 * j, j, 1, 4)

        return carry

    lax.fori_loop(0, heads, chain, 0)
    rows_ref[...] = tall[...].astype(jnp.bfloat16).reshape(tok, heads, dim)
    pltpu.make_async_copy(index_ref, idx_ref, index_sem).wait()

    def part(ref, h):
        return ref.at[pl.ds(h * half, half)]

    def climb_copy(source, slot, h):
        return pltpu.make_async_remote_copy(
            src_ref=part(source, h),
            dst_ref=part(climb.at[slot], h),
            send_sem=climb_send.at[slot, h],
            recv_sem=climb_recv.at[slot, h],
            device_id=(above, col),
            device_id_type=MESH,
        )

    def sink_copy(source, slot, h):
        return pltpu.make_async_remote_copy(
            src_ref=part(source, h),
            dst_ref=part(sink.at[slot], h),
            send_sem=sink_send.at[slot, h],
            recv_sem=sink_recv.at[slot, h],
            device_id=(below, col),
            device_id_type=MESH,
        )

    def distant_copy(source, target, h):
        return pltpu.make_async_remote_copy(
            src_ref=part(source, h),
            dst_ref=part(distant, h),
            send_sem=distant_send.at[h],
            recv_sem=distant_recv.at[h],
            device_id=(target, col),
            device_id_type=MESH,
        )

    for h in range(2):
        climb_copy(rows_ref, 1, h).start()
        sink_copy(rows_ref, 1, h).start()
    climb[0] = rows_ref[...]
    sink[0] = rows_ref[...]
    flat[pairs] = jnp.zeros(flat.shape[1:], jnp.bfloat16)
    got_up[0, pl.ds(half, half)] = jnp.zeros((half, mixed_ref.shape[1]), jnp.bfloat16)
    got_down[0, pl.ds(0, half)] = jnp.zeros((half, mixed_ref.shape[1]), jnp.bfloat16)

    def rows_to_wide(rows, count):
        tall[: count * heads, :] = rows.reshape(count * heads, dim).astype(jnp.float32)
        for j in range(heads):
            wide[:count, j * dim : (j + 1) * dim] = tall[
                pl.ds(j, count, stride=heads), :
            ].astype(jnp.bfloat16)

    def send_out(source, target, send_sem, recv_sem, p, i, each):
        other = lax.rem(col + i, columns)
        some = pl.ds(0, each)

        @pl.when(i == 0)
        def _():
            pltpu.make_async_copy(
                source.at[p, col, some], target.at[p, col, some], recv_sem.at[p]
            ).start()

        @pl.when(i > 0)
        def _():
            pltpu.make_async_remote_copy(
                src_ref=source.at[p, other, some],
                dst_ref=target.at[p, col, some],
                send_sem=send_sem.at[p],
                recv_sem=recv_sem.at[p],
                device_id=(seg, other),
                device_id_type=MESH,
            ).start()

    def wait_all(target, sem, p, each):
        piece = target.at[p, :, pl.ds(0, each)]
        pltpu.make_async_copy(piece, piece, sem.at[p]).wait()

    def wait_sent(source, sem, p, each):
        piece = source.at[p, pl.ds(0, columns - 1), pl.ds(0, each)]
        pltpu.make_async_copy(piece, piece, sem.at[p]).wait()

    def dispatch(p, each, slots):
        def one(i, carry):
            other = lax.rem(col + i, columns)
            for r in range(each):
                stage[p, other, r] = pick[r // 2, idx_ref[slots[r // 2], other, r % 2]]
            send_out(stage, arrive, stage_send, arrive_recv, p, i, each)
            return carry

        lax.fori_loop(0, columns, one, 0)

    def experts(p, each):
        count = columns * each
        wait_all(arrive, arrive_recv, p, each)
        wait_sent(stage, stage_send, p, each)
        rows_to_wide(arrive[p, :, :each].reshape(count, heads, dim), count)
        rows = wide[:count, :]
        gate_part = jnp.dot(rows, gate_ref[...], preferred_element_type=jnp.float32)
        up_part = jnp.dot(rows, up_ref[...], preferred_element_type=jnp.float32)
        hidden = (gate_part * jax.nn.sigmoid(gate_part) * up_part).astype(jnp.bfloat16)
        for j in range(heads):
            tall[pl.ds(j, count, stride=heads), :] = jnp.dot(
                hidden,
                down_ref[:, j * dim : (j + 1) * dim],
                preferred_element_type=jnp.float32,
            )
        stage[p, :, :each] = (
            tall[: count * heads, :].astype(jnp.bfloat16).reshape(columns, each, heads, dim)
        )

        def one(i, carry):
            send_out(stage, back, back_send, back_recv, p, i, each)
            return carry

        lax.fori_loop(0, columns, one, 0)

    def land(p, each):
        count = columns * each
        wait_all(back, back_recv, p, each)
        rows_to_wide(back[p, :, :each].reshape(count, heads, dim), count)
        flat[p, pl.ds(0, count)] = wide[:count, :]

    def gather_step(p, carry):
        for h in range(2):
            @pl.when(p >= 1)
            def _():
                climb_copy(rows_ref, p, h).wait_recv()

            @pl.when((p >= 1) & (p < pairs - 1))
            def _():
                climb_copy(climb.at[p], p + 1, h).start()

            @pl.when(p >= 1)
            def _():
                sink_copy(rows_ref, p, h).wait_recv()

            @pl.when((p >= 1) & (p < pairs - 1))
            def _():
                sink_copy(sink.at[p], p + 1, h).start()

            @pl.when(p == pairs - 1)
            def _():
                if h == 0:
                    distant_copy(climb.at[pairs - 1], above, 0).start()
                else:
                    distant_copy(sink.at[pairs - 1], below, 1).start()

        pick[0] = climb[p]
        pick[1] = sink[p]
        dispatch(p, 4, (jnp.maximum(2 * p - 1, 0), 2 * p))

        @pl.when(p == 1)
        def _():
            for k, (source, target) in enumerate(
                ((gate_in, gate_ref), (up_in, up_ref), (down_in, down_ref))
            ):
                load(source, target, k + 4).wait()

        @pl.when(p >= 1)
        def _():
            experts(p - 1, 4)

        @pl.when(p >= 2)
        def _():
            land(p - 2, 4)

        return carry

    lax.fori_loop(0, pairs, gather_step, 0)
    for h in range(2):
        distant_copy(rows_ref, above, h).wait_recv()
    pick[0] = distant[...]
    dispatch(pairs, 2, (segments - 1,))
    experts(pairs - 1, 4)
    land(pairs - 2, 4)
    experts(pairs, 2)
    land(pairs - 1, 4)
    land(pairs, 2)

    def term(p, source, h):
        weights = mix_ref[p, source, pl.ds(h * half, half), :]
        rows = flat[p]
        slots = rows.shape[0]
        return jnp.dot(
            weights[:, :slots], rows, preferred_element_type=jnp.float32
        ) + jnp.dot(weights[:, slots:], rows, preferred_element_type=jnp.float32)

    def up_copy(i, h):
        return pltpu.make_async_remote_copy(
            src_ref=part(sum_up.at[lax.rem(i, 2)], h),
            dst_ref=part(got_up.at[i], h),
            send_sem=up_send.at[i, h],
            recv_sem=up_recv.at[i, h],
            device_id=(above, col),
            device_id_type=MESH,
        )

    def down_copy(i, h):
        return pltpu.make_async_remote_copy(
            src_ref=part(sum_down.at[lax.rem(i, 2)], h),
            dst_ref=part(got_down.at[i], h),
            send_sem=down_send.at[i, h],
            recv_sem=down_recv.at[i, h],
            device_id=(below, col),
            device_id_type=MESH,
        )

    sum_up[0, pl.ds(0, half)] = term(pairs, 0, 0).astype(jnp.bfloat16)
    up_copy(0, 0).start()
    sum_down[0, pl.ds(half, half)] = term(pairs, 0, 1).astype(jnp.bfloat16)
    down_copy(0, 1).start()

    def reduce_step(i, carry):
        for h in range(2):
            spot = pl.ds(h * half, half)
            mine = term(pairs - i, 1, h)

            @pl.when((i > 1) | (h == 0))
            def _():
                up_copy(i - 1, h).wait_recv()


            @pl.when((i > 2) | ((i == 2) & (h == 0)))
            def _():
                up_copy(i - 2, h).wait_send()

            sum_up[lax.rem(i, 2), spot] = (mine + got_up[i - 1, spot].astype(jnp.float32)).astype(
                jnp.bfloat16
            )
            up_copy(i, h).start()
            mine = term(pairs - i, 0, h)

            @pl.when((i > 1) | (h == 1))
            def _():
                down_copy(i - 1, h).wait_recv()


            @pl.when((i > 2) | ((i == 2) & (h == 1)))
            def _():
                down_copy(i - 2, h).wait_send()

            sum_down[lax.rem(i, 2), spot] = (
                mine + got_down[i - 1, spot].astype(jnp.float32)
            ).astype(jnp.bfloat16)
            down_copy(i, h).start()

        return carry

    lax.fori_loop(1, pairs, reduce_step, 0)
    for h in range(2):
        spot = pl.ds(h * half, half)
        total = mixed_ref[spot, :].astype(jnp.float32) + term(0, 0, h)
        up_copy(pairs - 1, h).wait_recv()
        total = total + got_up[pairs - 1, spot].astype(jnp.float32)
        down_copy(pairs - 1, h).wait_recv()
        total = total + got_down[pairs - 1, spot].astype(jnp.float32)
        out_ref[spot, :] = total.astype(jnp.bfloat16)

    def drain(p, carry):
        wait_sent(stage, back_send, p, 4)
        for h in range(2):

            @pl.when(p >= 1)
            def _():
                climb_copy(rows_ref, p, h).wait_send()
                sink_copy(rows_ref, p, h).wait_send()

            @pl.when(p >= pairs - 2)
            def _():
                up_copy(p, h).wait_send()
                down_copy(p, h).wait_send()

        return carry

    lax.fori_loop(0, pairs, drain, 0)
    wait_sent(stage, back_send, pairs, 2)
    for h in range(2):
        distant_copy(rows_ref, above, h).wait_send()
    pltpu.make_async_copy(final_ref, final_ref, final_recv).wait()

    for r in range(cached):
        replaced = jnp.where(slot_ref[0] == r, 1.0, 0.0)
        store_out_ref[r, 0] = (
            final_ref[:, :dim].astype(jnp.float32) * replaced
            + store_ref[r, 0].astype(jnp.float32) * (1.0 - replaced)
        ).astype(jnp.bfloat16)

    def routes_sent(k, carry):
        routes_copy(k, 2 * k - 1).wait_send()
        routes_copy(segments - k, 2 * k).wait_send()
        return carry

    lax.fori_loop(1, far, routes_sent, 0)
    routes_copy(far, segments - 1).wait_send()
    sent = offer.at[pl.ds(0, columns - 1)]
    pltpu.make_async_copy(sent, sent, offer_send).wait()

    @pl.when(seg > 0)
    def _():
        origin_copy().wait_send()

    def drain(j, carry):
        @pl.when(seg < segments - 1)
        def _():
            hand_on(j, 0).wait_send()

        @pl.when((seg == segments - 1) & (j < segments - 1))
        def _():
            end_copy(j).wait_send()

        return carry

    lax.fori_loop(0, heads, drain, 0)


def mixer(lengths, places, slots, beta, decay, gain, ids, weights, store, k, q, v, w_gate, w_up, w_down):
    segments = lax.axis_size("segment")
    columns = lax.axis_size("expert")
    pairs = segments // 2
    heads = segments
    tok, width = v.shape
    dim = store.shape[-1]
    top = ids.shape[0]
    bf, f32 = jnp.bfloat16, jnp.float32
    dma = pltpu.SemaphoreType.DMA
    whole = pl.BlockSpec(memory_space=pltpu.VMEM)
    scalars = pl.BlockSpec(memory_space=pltpu.SMEM)
    remote = pl.BlockSpec(memory_space=pl.ANY)
    return pl.pallas_call(
        mixer_kernel,
        out_shape=(
            jax.ShapeDtypeStruct((tok, width), bf),
            jax.ShapeDtypeStruct(store.shape, bf),
        ),
        in_specs=[scalars] * 3 + [whole] * 5 + [remote] * 7,
        out_specs=(whole, whole),
        scratch_shapes=[
            pltpu.VMEM(store.shape, bf),
            pltpu.VMEM(k.shape, bf),
            pltpu.VMEM(q.shape, bf),
            pltpu.VMEM(v.shape, bf),
            pltpu.VMEM(w_gate.shape, bf),
            pltpu.VMEM(w_up.shape, bf),
            pltpu.VMEM(w_down.shape, bf),
            pltpu.VMEM((2 * top, tok), f32),
            pltpu.VMEM((segments, 2 * top, tok), f32),
            pltpu.VMEM((segments, columns, tok), jnp.int32),
            pltpu.SMEM((segments, columns, tok), jnp.int32),
            pltpu.VMEM((pairs + 1, 2, tok, 2 * tok), bf),
            pltpu.VMEM((tok, tok), f32),
            pltpu.VMEM((tok, width), bf),
            pltpu.VMEM((tok, heads, dim), bf),
            pltpu.VMEM((dim, 2 * dim), bf),
            pltpu.VMEM((columns, dim, dim), bf),
            pltpu.VMEM((columns, dim, dim), bf),
            pltpu.VMEM((dim, 2 * dim), bf),
            pltpu.VMEM((heads, dim, 2 * dim), bf),
            pltpu.VMEM((heads, dim, 2 * dim), bf),
            pltpu.VMEM((heads, 2 * dim, 2 * dim), bf),
            pltpu.VMEM((heads, 2 * dim, dim), f32),
            pltpu.VMEM((tok, heads), f32),
            pltpu.VMEM((tok, heads), f32),
            pltpu.VMEM((heads, tok), f32),
            pltpu.VMEM((pairs, tok, heads, dim), bf),
            pltpu.VMEM((pairs, tok, heads, dim), bf),
            pltpu.VMEM((tok, heads, dim), bf),
            pltpu.VMEM((2, tok, heads, dim), bf),
            pltpu.VMEM((pairs + 1, columns, 4, heads, dim), bf),
            pltpu.VMEM((pairs + 1, columns, 4, heads, dim), bf),
            pltpu.VMEM((pairs + 1, columns, 4, heads, dim), bf),
            pltpu.VMEM((pairs + 1, columns * 4, width), bf),
            pltpu.VMEM((2, tok, width), bf),
            pltpu.VMEM((2, tok, width), bf),
            pltpu.VMEM((pairs, tok, width), bf),
            pltpu.VMEM((pairs, tok, width), bf),
            pltpu.VMEM((tok * heads, dim), f32),
            pltpu.VMEM((tok, width), bf),
            dma((7,)),
            dma((segments,)),
            dma,
            dma,
            dma,
            dma,
            dma,
            dma((heads,)),
            dma((heads,)),
            dma((heads,)),
            dma,
            dma((2,)),
            dma((2,)),
            dma((pairs, 2)),
            dma((pairs, 2)),
            dma((pairs, 2)),
            dma((pairs, 2)),
            dma((pairs + 1,)),
            dma((pairs + 1,)),
            dma((pairs + 1,)),
            dma((pairs + 1,)),
            dma((pairs, 2)),
            dma((pairs, 2)),
            dma((pairs, 2)),
            dma((pairs, 2)),
        ],
        compiler_params=pltpu.CompilerParams(
            collective_id=1, has_side_effects=True, vmem_limit_bytes=62 * 1024 * 1024
        ),
    )(lengths, places, slots, beta, decay, gain, ids, weights, store, k, q, v, w_gate, w_up, w_down)


def shards(
    q_heads,
    k_heads,
    values,
    beta,
    decay,
    head_gain,
    suffix_len,
    store_states,
    cache_row,
    write_slot,
    expert_ids,
    route_weight,
    w_gate,
    w_up,
    w_down,
):
    out, store_out = mixer(
        suffix_len,
        cache_row,
        write_slot,
        beta[0].T,
        decay[0].T,
        head_gain.reshape(1, -1),
        expert_ids[0].T,
        route_weight[0].T,
        store_states,
        k_heads[0],
        q_heads[0],
        values[0],
        w_gate[0],
        w_up[0],
        w_down[0],
    )
    return (out[None], store_out)


def solution(mesh):
    return jax.shard_map(
        shards,
        mesh=mesh,
        in_specs=(
            P("expert", "segment", None),
            P("expert", "segment", None),
            P("expert", "segment", None),
            P("expert", "segment", None),
            P("expert", "segment", None),
            P(),
            P("expert"),
            P("expert", "segment", None, None),
            P(),
            P("expert"),
            P("expert", "segment", None),
            P("expert", "segment", None),
            P(("segment", "expert"), None, None),
            P(("segment", "expert"), None, None),
            P(("segment", "expert"), None, None),
        ),
        out_specs=(P("expert", "segment", None), P("expert", "segment", None, None)),
        check_vma=False,
    )
```

time: 394 us -> 325 us (0.82)
  blocking collectives: 29.6 us -> 0 us
  Pallas kernels: 349 us -> 320 us
  local copies, waits for them, and re-layouts: 8.69 us -> 2.58 us
  other arithmetic: 4.06 us -> 0 us
    all_gather x1 -> x0, blocking collectives: 29.6 us -> none  [route_tables(): routes = lax.all_gather(routes, 'segment', axis=0, tiled=False)]
    pallas_call x2 -> x1, Pallas kernels: 349 us -> 320 us  [mixer(): pl.pallas_call(mixer_kernel, out_shape=(jax.ShapeDtypeStruct((tok, width)...]
    unnamed x22 -> x4, local copies, waits for them, and re-layouts: 6.59 us -> 2.58 us
where the time goes in v3:
time: 325 us
  Pallas kernels  320 us (98%)
    pallas_call x1, Pallas kernels, mixer(): pl.pallas_call(mixer_kernel, out_shape=(jax.ShapeDtypeStruct((tok, width)...  320 us

profile of v3, /device:TPU:1, one launch (start us, length us, event | category | flops | bytes accessed | tf_op | source)
XLA Modules:
  0.0 325.0 jit_solution(9651242768614511649)
XLA Ops:
  1.9 320.4 %shard_map.158 = (bf16[128,2048]{1,0:T(8,128)(2,1)}, bf16[4,1,128,128]{3,2,1,0:T(8,128)(2,1)}) custom-call(s32[1]{0:T(128)S(6)} %copy.19.len_ref, s32[32]{0:T(128)} %row_ref.1, s32[1]{0:T(128)S(6)} %copy.20.slot_ref, bf16[16,128]{1,0:T(8,128)(2,1)} %bitcast.27, bf16[16,128]{1,0:T(8,128)(2,1)} %bitcast.28, f32[1,128]{1,0:T(1,128)} %bitcast.31, ...), custom_call_target="tpu_custom_call" | custom-call | tf_op jit(solution)/shard_map/pallas_call | solution.py:783
  322.4 0.0 copy-start
  322.4 1.9 copy.21
  324.3 0.0 copy-done
  324.3 0.7 copy.22
Async XLA Ops:
  322.4 1.9 copy-start

commit v4 on v3

--- a/solution.py
+++ b/solution.py
@@ -9,6 +9,8 @@
 
 
 GROUP = 4
+UNROLL = 5
+PARTS = 4
 
 
 def halves(block):
@@ -69,7 +71,6 @@
     index_ref,
     idx_ref,
     mix_ref,
-    spread_ref,
     mixed_ref,
     rows_ref,
     final_ref,
@@ -78,7 +79,8 @@
     origin,
     held,
     passed,
-    step_left,
+    step_right,
+    step_read,
     step_add,
     strength_ref,
     total_ref,
@@ -193,16 +195,21 @@
     lax.fori_loop(1, far, routes_out, 0)
     routes_copy(far, segments - 1).start()
 
+    @pl.when(seg == 0)
+    def _():
+        held[:, :, dim:] = jnp.zeros((heads, dim, dim), jnp.bfloat16)
+
     load(store_in, store_ref, 0).wait()
 
     def propose(i, carry):
         other = lax.rem(col + i, columns)
         wanted = row_ref[other]
-        block = jnp.zeros((dim, dim), jnp.float32)
+        block = jnp.zeros((dim, dim), jnp.bfloat16)
         for r in range(cached):
             match = jnp.where(wanted == col * cached + r, 1.0, 0.0)
-            block = block + store_ref[r, 0].astype(jnp.float32) * match
-        offer[other] = block.astype(jnp.bfloat16)
+            match = jnp.full((dim, dim), match, jnp.float32).astype(jnp.bfloat16)
+            block = block + store_ref[r, 0] * match
+        offer[other] = block
 
         @pl.when(i == 0)
         def _():
@@ -318,21 +325,24 @@
             scores = upto[a] * grams[a // share][tok:]
             left = left_pair(jnp.concatenate([tail, scores], axis=0))
             minus = paired_dot(left, weights[a])
-            step_add[number[a]] = paired_dot(left, pseudo[a])
-            step_left[number[a]] = left_pair(
-                jnp.concatenate(
-                    [jnp.exp(last) * identity, growth[a] * unit_queries[a // share]], axis=0
-                )
-                - minus
-            )
-        return carry
-
-    def hand_on(j, carry):
+            plus = paired_dot(left, pseudo[a])
+            step_right[number[a]] = right_pair((jnp.exp(last) * identity - minus[:dim]).T)
+            step_add[number[a], :dim] = plus[:dim].T
+            step_add[number[a], dim:] = plus[dim:]
+            high, low = halves(growth[a] * unit_queries[a // share] - minus[dim:])
+            read = jnp.concatenate([high, low], axis=0)
+            step_read[number[a]] = jnp.concatenate([read, read], axis=1)
+        return carry
+
+    rows_each = dim // PARTS
+
+    def hand_on(j, h):
+        some = pl.ds(h * rows_each, rows_each)
         return pltpu.make_async_remote_copy(
-            src_ref=passed.at[j],
-            dst_ref=held.at[j],
-            send_sem=passed_send.at[j],
-            recv_sem=held_recv.at[j],
+            src_ref=passed.at[j, some],
+            dst_ref=held.at[j, some],
+            send_sem=passed_send.at[j, h],
+            recv_sem=held_recv.at[j, h],
             device_id=(seg + 1, col),
             device_id_type=MESH,
         )
@@ -340,9 +350,9 @@
     def origin_copy():
         return pltpu.make_async_remote_copy(
             src_ref=origin,
-            dst_ref=held.at[seg],
+            dst_ref=held.at[seg, :, pl.ds(0, dim)],
             send_sem=origin_send,
-            recv_sem=held_recv.at[seg],
+            recv_sem=held_recv.at[seg, 0],
             device_id=(0, col),
             device_id_type=MESH,
         )
@@ -364,27 +374,17 @@
             return block + taken[i].astype(jnp.float32)
 
         block = lax.fori_loop(0, columns, add_up, jnp.zeros((dim, dim), jnp.float32))
-        origin[:, :dim] = block.astype(jnp.bfloat16)
-        origin[:, dim:] = jnp.zeros((dim, dim), jnp.bfloat16)
+        origin[...] = block.T.astype(jnp.bfloat16)
 
         @pl.when(seg == 0)
         def _():
-            pltpu.make_async_copy(origin, held.at[0], held_recv.at[0]).start()
+            pltpu.make_async_copy(origin, held.at[0, :, pl.ds(0, dim)], held_recv.at[0, 0]).start()
 
         @pl.when(seg > 0)
         def _():
             origin_copy().start()
 
-    def local_step(i, carry):
-        local_work(i, carry)
-
-        @pl.when(i == heads // share // GROUP // 2)
-        def _():
-            give_origin()
-
-        return carry
-
-    lax.fori_loop(0, heads // share // GROUP, local_step, 0)
+    lax.fori_loop(0, heads // share // GROUP, local_work, 0)
 
     names = lax.broadcasted_iota(jnp.int32, (columns, 1), 0) + seg * columns
     token = lax.broadcasted_iota(jnp.int32, (columns, tok), 1)
@@ -410,19 +410,33 @@
 
     def tabulate(slot, p, source, width):
         at_first, at_last = locate(slot)
-        spread_ref[...] = jnp.zeros_like(spread_ref)
-        spread_ref[pl.ds(2 * source, columns, stride=width), :] = at_first
-        spread_ref[pl.ds(2 * source + 1, columns, stride=width), :] = at_last
-        mix_ref[p, source] = left_pair(spread_ref[...].T)
+        tall[:tok] = jnp.zeros((tok, tok), jnp.float32)
+        tall[pl.ds(2 * source, columns, stride=width), :] = at_first
+        tall[pl.ds(2 * source + 1, columns, stride=width), :] = at_last
+        mix_ref[p, source] = left_pair(tall[:tok].T)
 
     def chain(j, carry):
-        pltpu.make_async_copy(held.at[j], held.at[j], held_recv.at[j]).wait()
-        state = jnp.concatenate([held[j], held[j]], axis=0)
-        passed[j] = left_pair(paired_dot(step_left[j, :dim], state) + step_add[j, :dim])
-
-        @pl.when(seg < segments - 1)
-        def _():
-            hand_on(j, 0).start()
+        for h in range(PARTS):
+            some = pl.ds(h * rows_each, rows_each)
+            if h == 0:
+
+                @pl.when(seg == 0)
+                def _():
+                    piece = held.at[j, :, pl.ds(0, dim)]
+                    pltpu.make_async_copy(piece, piece, held_recv.at[j, 0]).wait()
+
+            @pl.when(seg > 0)
+            def _():
+                piece = held.at[j, some]
+                pltpu.make_async_copy(piece, piece, held_recv.at[j, h]).wait()
+
+            passed[j, some] = left_pair(
+                paired_dot(held[j, some], step_right[j]) + step_add[j, some]
+            )
+
+            @pl.when(seg < segments - 1)
+            def _():
+                hand_on(j, h).start()
 
         @pl.when((seg == segments - 1) & (j < segments - 1))
         def _():
@@ -432,25 +446,26 @@
         def _():
             pltpu.make_async_copy(passed.at[j], final_ref, final_recv).start()
 
-        raw = (paired_dot(step_left[j, dim:], state) + step_add[j, dim:]) * valid
+        both = lax.dot_general(
+            step_read[j], held[j], turned, preferred_element_type=jnp.float32
+        )
+        raw = (both[:tok] + both[tok:] + step_add[j, dim:]) * valid
         squares = jnp.sum(raw * raw, axis=-1, keepdims=True) * (1.0 / dim)
         normed = raw * lax.rsqrt(squares + 1e-06) * gain_ref[...]
         mixed_ref[:, pl.ds(pl.multiple_of(j * dim, dim), dim)] = normed.astype(jnp.bfloat16)
         tall[pl.ds(j, tok, stride=heads), :] = normed
-
-        @pl.when(j == 0)
-        def _():
-            pltpu.make_async_copy(routes_all, routes_all, routes_recv).wait()
-            tabulate(0, 0, 0, 4)
-            tabulate(segments - 1, far, 0, 2)
-
-        @pl.when((j > 0) & (j < far))
-        def _():
-            tabulate(2 * j - 1, j, 0, 4)
-            tabulate(2 * j, j, 1, 4)
-
-        return carry
-
+        return carry
+
+    def tables(k, carry):
+        tabulate(2 * k - 1, k, 0, 4)
+        tabulate(2 * k, k, 1, 4)
+        return carry
+
+    pltpu.make_async_copy(routes_all, routes_all, routes_recv).wait()
+    tabulate(0, 0, 0, 4)
+    tabulate(segments - 1, far, 0, 2)
+    give_origin()
+    lax.fori_loop(1, far, tables, 0)
     lax.fori_loop(0, heads, chain, 0)
     rows_ref[...] = tall[...].astype(jnp.bfloat16).reshape(tok, heads, dim)
     pltpu.make_async_copy(index_ref, idx_ref, index_sem).wait()
@@ -504,26 +519,33 @@
                 pl.ds(j, count, stride=heads), :
             ].astype(jnp.bfloat16)
 
-    def send_out(source, target, send_sem, recv_sem, p, i, each):
-        other = lax.rem(col + i, columns)
+    def to_all(step):
+        def some_of(i, carry):
+            for u in range(UNROLL):
+                step(1 + i * UNROLL + u)
+            return carry
+
+        rounds = (columns - 1) // UNROLL
+        lax.fori_loop(0, rounds, some_of, 0)
+        for rest in range(1 + rounds * UNROLL, columns):
+            step(rest)
+
+    def keep_own(source, target, recv_sem, p, each):
         some = pl.ds(0, each)
-
-        @pl.when(i == 0)
-        def _():
-            pltpu.make_async_copy(
-                source.at[p, col, some], target.at[p, col, some], recv_sem.at[p]
-            ).start()
-
-        @pl.when(i > 0)
-        def _():
-            pltpu.make_async_remote_copy(
-                src_ref=source.at[p, other, some],
-                dst_ref=target.at[p, col, some],
-                send_sem=send_sem.at[p],
-                recv_sem=recv_sem.at[p],
-                device_id=(seg, other),
-                device_id_type=MESH,
-            ).start()
+        pltpu.make_async_copy(
+            source.at[p, col, some], target.at[p, col, some], recv_sem.at[p]
+        ).start()
+
+    def send_out(source, target, send_sem, recv_sem, p, other, each):
+        some = pl.ds(0, each)
+        pltpu.make_async_remote_copy(
+            src_ref=source.at[p, other, some],
+            dst_ref=target.at[p, col, some],
+            send_sem=send_sem.at[p],
+            recv_sem=recv_sem.at[p],
+            device_id=(seg, other),
+            device_id_type=MESH,
+        ).start()
 
     def wait_all(target, sem, p, each):
         piece = target.at[p, :, pl.ds(0, each)]
@@ -534,14 +556,18 @@
         pltpu.make_async_copy(piece, piece, sem.at[p]).wait()
 
     def dispatch(p, each, slots):
-        def one(i, carry):
-            other = lax.rem(col + i, columns)
+        def choose(other):
             for r in range(each):
                 stage[p, other, r] = pick[r // 2, idx_ref[slots[r // 2], other, r % 2]]
-            send_out(stage, arrive, stage_send, arrive_recv, p, i, each)
-            return carry
-
-        lax.fori_loop(0, columns, one, 0)
+
+        def step(i):
+            other = lax.rem(col + i, columns)
+            choose(other)
+            send_out(stage, arrive, stage_send, arrive_recv, p, other, each)
+
+        to_all(step)
+        choose(col)
+        keep_own(stage, arrive, arrive_recv, p, each)
 
     def experts(p, each):
         count = columns * each
@@ -562,11 +588,11 @@
             tall[: count * heads, :].astype(jnp.bfloat16).reshape(columns, each, heads, dim)
         )
 
-        def one(i, carry):
-            send_out(stage, back, back_send, back_recv, p, i, each)
-            return carry
-
-        lax.fori_loop(0, columns, one, 0)
+        def step(i):
+            send_out(stage, back, back_send, back_recv, p, lax.rem(col + i, columns), each)
+
+        to_all(step)
+        keep_own(stage, back, back_recv, p, each)
 
     def land(p, each):
         count = columns * each
@@ -732,10 +758,11 @@
         distant_copy(rows_ref, above, h).wait_send()
     pltpu.make_async_copy(final_ref, final_ref, final_recv).wait()
 
+    checkpoint = final_ref[:, :dim].astype(jnp.float32).T
     for r in range(cached):
         replaced = jnp.where(slot_ref[0] == r, 1.0, 0.0)
         store_out_ref[r, 0] = (
-            final_ref[:, :dim].astype(jnp.float32) * replaced
+            checkpoint * replaced
             + store_ref[r, 0].astype(jnp.float32) * (1.0 - replaced)
         ).astype(jnp.bfloat16)
 
@@ -756,7 +783,8 @@
     def drain(j, carry):
         @pl.when(seg < segments - 1)
         def _():
-            hand_on(j, 0).wait_send()
+            for h in range(PARTS):
+                hand_on(j, h).wait_send()
 
         @pl.when((seg == segments - 1) & (j < segments - 1))
         def _():
@@ -801,15 +829,15 @@
             pltpu.VMEM((segments, columns, tok), jnp.int32),
             pltpu.SMEM((segments, columns, tok), jnp.int32),
             pltpu.VMEM((pairs + 1, 2, tok, 2 * tok), bf),
-            pltpu.VMEM((tok, tok), f32),
             pltpu.VMEM((tok, width), bf),
             pltpu.VMEM((tok, heads, dim), bf),
             pltpu.VMEM((dim, 2 * dim), bf),
             pltpu.VMEM((columns, dim, dim), bf),
             pltpu.VMEM((columns, dim, dim), bf),
-            pltpu.VMEM((dim, 2 * dim), bf),
+            pltpu.VMEM((dim, dim), bf),
             pltpu.VMEM((heads, dim, 2 * dim), bf),
             pltpu.VMEM((heads, dim, 2 * dim), bf),
+            pltpu.VMEM((heads, 2 * dim, 2 * dim), bf),
             pltpu.VMEM((heads, 2 * dim, 2 * dim), bf),
             pltpu.VMEM((heads, 2 * dim, dim), f32),
             pltpu.VMEM((tok, heads), f32),
@@ -836,8 +864,8 @@
             dma,
             dma,
             dma,
-            dma((heads,)),
-            dma((heads,)),
+            dma((heads, PARTS)),
+            dma((heads, PARTS)),
             dma((heads,)),
             dma,
             dma((2,)),

time: 325 us -> 309 us (0.951)
  Pallas kernels: 320 us -> 303 us
    pallas_call x1, Pallas kernels: 320 us -> 303 us  [mixer(): pl.pallas_call(mixer_kernel, out_shape=(jax.ShapeDtypeStruct((tok, width)...]
where the time goes in v4:
time: 309 us; the launch traced here: 308 us
  Pallas kernels  303 us (98%)
    pallas_call x1, Pallas kernels, mixer(): pl.pallas_call(mixer_kernel, out_shape=(jax.ShapeDtypeStruct((tok, width)...  303 us

profile of v4, /device:TPU:1, one launch (start us, length us, event | category | flops | bytes accessed | tf_op | source)
XLA Modules:
  0.0 307.6 jit_solution(11062185687063013583)
XLA Ops:
  1.9 303.1 %shard_map.158 = (bf16[128,2048]{1,0:T(8,128)(2,1)}, bf16[4,1,128,128]{3,2,1,0:T(8,128)(2,1)}) custom-call(s32[1]{0:T(128)S(6)} %copy.19.len_ref, s32[32]{0:T(128)} %row_ref.1, s32[1]{0:T(128)S(6)} %copy.20.slot_ref, bf16[16,128]{1,0:T(8,128)(2,1)} %bitcast.27, bf16[16,128]{1,0:T(8,128)(2,1)} %bitcast.28, f32[1,128]{1,0:T(1,128)} %bitcast.31, ...), custom_call_target="tpu_custom_call" | custom-call | tf_op jit(solution)/shard_map/pallas_call | solution.py:811
  305.0 0.0 copy-start
  305.0 1.9 copy.21
  306.9 0.0 copy-done
  306.9 0.7 copy.22
Async XLA Ops:
  305.0 1.9 copy-start

commit v5 on v4

--- a/solution.py
+++ b/solution.py
@@ -505,7 +505,7 @@
 
     for h in range(2):
         climb_copy(rows_ref, 1, h).start()
-        sink_copy(rows_ref, 1, h).start()
+        sink_copy(rows_ref, 1, 1 - h).start()
     climb[0] = rows_ref[...]
     sink[0] = rows_ref[...]
     flat[pairs] = jnp.zeros(flat.shape[1:], jnp.bfloat16)
@@ -612,17 +612,17 @@
 
             @pl.when(p >= 1)
             def _():
-                sink_copy(rows_ref, p, h).wait_recv()
+                sink_copy(rows_ref, p, 1 - h).wait_recv()
 
             @pl.when((p >= 1) & (p < pairs - 1))
             def _():
-                sink_copy(sink.at[p], p + 1, h).start()
-
-            @pl.when(p == pairs - 1)
-            def _():
-                if h == 0:
+                sink_copy(sink.at[p], p + 1, 1 - h).start()
+
+            if h == 0:
+
+                @pl.when(p == pairs - 1)
+                def _():
                     distant_copy(climb.at[pairs - 1], above, 0).start()
-                else:
                     distant_copy(sink.at[pairs - 1], below, 1).start()
 
         pick[0] = climb[p]
@@ -692,37 +692,37 @@
 
     def reduce_step(i, carry):
         for h in range(2):
-            spot = pl.ds(h * half, half)
-            mine = term(pairs - i, 1, h)
-
-            @pl.when((i > 1) | (h == 0))
-            def _():
-                up_copy(i - 1, h).wait_recv()
-
-
-            @pl.when((i > 2) | ((i == 2) & (h == 0)))
-            def _():
-                up_copy(i - 2, h).wait_send()
+            rise, fall = 1 - h, h
+            spot = pl.ds(rise * half, half)
+            mine = term(pairs - i, 1, rise)
+
+            @pl.when((i > 1) | (rise == 0))
+            def _():
+                up_copy(i - 1, rise).wait_recv()
+
+            @pl.when((i > 2) | ((i == 2) & (rise == 0)))
+            def _():
+                up_copy(i - 2, rise).wait_send()
 
             sum_up[lax.rem(i, 2), spot] = (mine + got_up[i - 1, spot].astype(jnp.float32)).astype(
                 jnp.bfloat16
             )
-            up_copy(i, h).start()
-            mine = term(pairs - i, 0, h)
-
-            @pl.when((i > 1) | (h == 1))
-            def _():
-                down_copy(i - 1, h).wait_recv()
-
-
-            @pl.when((i > 2) | ((i == 2) & (h == 1)))
-            def _():
-                down_copy(i - 2, h).wait_send()
+            up_copy(i, rise).start()
+            spot = pl.ds(fall * half, half)
+            mine = term(pairs - i, 0, fall)
+
+            @pl.when((i > 1) | (fall == 1))
+            def _():
+                down_copy(i - 1, fall).wait_recv()
+
+            @pl.when((i > 2) | ((i == 2) & (fall == 1)))
+            def _():
+                down_copy(i - 2, fall).wait_send()
 
             sum_down[lax.rem(i, 2), spot] = (
                 mine + got_down[i - 1, spot].astype(jnp.float32)
             ).astype(jnp.bfloat16)
-            down_copy(i, h).start()
+            down_copy(i, fall).start()
 
         return carry
 

time: 309 us -> 307 us (level)
  no operation moved by 1% of the time
where the time goes in v5:
time: 307 us
  Pallas kernels  303 us (99%)
    pallas_call x1, Pallas kernels, mixer(): pl.pallas_call(mixer_kernel, out_shape=(jax.ShapeDtypeStruct((tok, width)...  303 us

profile of v5, /device:TPU:1, one launch (start us, length us, event | category | flops | bytes accessed | tf_op | source)
XLA Modules:
  0.0 307.1 jit_solution(10336262239310333728)
XLA Ops:
  1.9 302.6 %shard_map.158 = (bf16[128,2048]{1,0:T(8,128)(2,1)}, bf16[4,1,128,128]{3,2,1,0:T(8,128)(2,1)}) custom-call(s32[1]{0:T(128)S(6)} %copy.19.len_ref, s32[32]{0:T(128)} %row_ref.1, s32[1]{0:T(128)S(6)} %copy.20.slot_ref, bf16[16,128]{1,0:T(8,128)(2,1)} %bitcast.27, bf16[16,128]{1,0:T(8,128)(2,1)} %bitcast.28, f32[1,128]{1,0:T(1,128)} %bitcast.31, ...), custom_call_target="tpu_custom_call" | custom-call | tf_op jit(solution)/shard_map/pallas_call | solution.py:811
  304.5 0.0 copy-start
  304.5 1.9 copy.21
  306.5 0.0 copy-done
  306.5 0.7 copy.22
Async XLA Ops:
  304.5 1.9 copy-start
